TPU v7x, 512 devices: a whole 4x8x8 slice. The times are simulated.
512 devices in a mesh: mode: 16 (over y, core), cell: 32 (over z, x).
Axes of the slice: x: 4, y: 8, z: 8, core: 2. Of those that a mesh axis runs over, the one named last changes fastest.
Arguments:
- initial: float32 [1536, 64, 2048], P('mode', 'cell'), may hold values from -6 to 6
- scatter_matrix: bfloat16 [1536, 1536], replicated, may hold values from -0.15625 to 0.15625
- speed_x: float32 [1536], P('mode'), may hold values from -1 to 1
- speed_y: float32 [1536], P('mode'), may hold values from -1 to 1
- relaxation: float32 [1536], P('mode'), may hold values from 0.5 to 4
- emission: float32 [1536], P('mode'), may hold values from -4 to 4
- heater: int32 [64, 2048], P('cell'), may hold values 0 or 1
Outputs:
- distribution: float32 [1536, 64, 2048], P('mode', 'cell')
All inputs are finite; a program needn't handle non-finite values. No bound on the sum of `heater` on one device may be relied on, other than what follows from the above.
Results may differ from a plain program's by a relative error of at most 0.0026.
Values may be sent and summed in bfloat16 or wider, within the bound.
No kernel may reach another device: no remote copies, remote signals or barrier semaphores. Data moves between devices by JAX's collectives and lax.ppermute only.
A program may use at most 64 MiB of HBM per device.

v0:
```python
import jax
import jax.numpy as jnp
from jax import lax
from jax.sharding import PartitionSpec as P

ITERS = 2


def padded_2(cells, sides, width):
    for axis, dim in sides:
        count = lax.axis_size(axis)
        ends = count - 1
        head = lax.slice_in_dim(cells, 0, width, axis=dim)
        tail = lax.slice_in_dim(cells, cells.shape[dim] - width, cells.shape[dim], axis=dim)
        cells = jnp.concatenate(
            [
                lax.ppermute(tail, axis, [(i, (i + 1) % count) for i in range(ends)]),
                cells,
                lax.ppermute(head, axis, [((i + 1) % count, i) for i in range(ends)]),
            ],
            axis=dim,
        )
    return cells


def stream_y(field, speed_y):
    padded = jnp.pad(field, ((0, 0), (0, 0), (1, 1)))
    return jnp.where(speed_y[:, None, None] > 0, padded[:, :, :-2], padded[:, :, 2:])


def apply_matrix(scatter_matrix, block):
    return jnp.einsum("ij,jkc->ikc", scatter_matrix, block, preferred_element_type=jnp.float32)


def shards(initial, scatter_matrix, speed_x, speed_y, relaxation, emission, heater):
    rate_x = jnp.abs(speed_x)[:, None, None]
    rate_y = jnp.abs(speed_y)[:, None, None]
    denominator = relaxation[:, None, None] + rate_x + rate_y
    source = heater.astype(jnp.float32)[None, :, :] * emission[:, None, None]
    field = initial
    for step in range(ITERS):
        narrow = field.astype(jnp.bfloat16)
        complete = apply_matrix(
            scatter_matrix, lax.all_to_all(narrow, "mode", split_axis=2, concat_axis=0, tiled=True)
        )
        scattered = lax.all_to_all(complete, "mode", split_axis=0, concat_axis=2, tiled=True)
        padded = padded_2(field, (("cell", 1),), 1)
        from_x = jnp.where(speed_x[:, None, None] > 0, padded[:, :-2, :], padded[:, 2:, :])
        from_y = stream_y(field, speed_y)
        field = (rate_x * from_x + rate_y * from_y + scattered + source) / denominator
    return field


def solution(mesh):
    return jax.shard_map(
        shards,
        mesh=mesh,
        in_specs=(
            P("mode", "cell", None),
            P(),
            P("mode"),
            P("mode"),
            P("mode"),
            P("mode"),
            P("cell", None),
        ),
        out_specs=P("mode", "cell", None),
        check_vma=False,
    )
```

profile of v0, /device:TPU:1, one launch (start us, length us, event | category | flops | bytes accessed | tf_op | source)
XLA Modules:
  0.0 192.4 jit_solution(7217708215785034765)
XLA Ops:
  0.0 2.2 %copy.87 = bf16[96,2,2048]{2,0,1:T(8,128)(2,1)S(1)} copy(f32[96,2,2048]{2,1,0:T(2,128)} %param.7) | data formatting | bytes 2359296 | tf_op args[0]
  2.3 0.8 copy.68
  3.0 37.9 %all_to_all.72 = bf16[96,2,2048]{0,1,2:T(2,128)(2,1)S(1)} all-to-all(bf16[96,2,2048]{0,1,2:T(2,128)(2,1)S(1)} %copy.68), channel_id=1, replica_groups=mesh['mode'=16,'cell'=32] {'mode'}, dimensions={2} | all-to-all | bytes 1572864 | tf_op jit(solution)/shard_map/all_to_all | solution.py:44
  40.9 0.8 copy.69
  41.8 3.7 %fusion.2 = f32[1536,2,128]{2,0,1:T(8,128)S(1)} fusion(bf16[1536,2,128]{2,0,1:T(8,128)(2,1)S(1)} %bitcast.38, bf16[1536,1536]{1,0:T(8,128)(2,1)} %param.8), kind=kOutput, calls=%fused_computation.2 | convolution fusion | flops 1207959552 | bytes 7077888 | tf_op jit(solution)/shard_map/ij,jkc->ikc/dot_general | solution.py:32
  45.5 6.6 %copy.70 = f32[1536,2,128]{2,1,0:T(2,128)} copy(f32[1536,2,128]{2,0,1:T(8,128)S(1)} %fusion.2) | data formatting | bytes 3145728 | tf_op jit(solution)/shard_map/ij,jkc->ikc/dot_general | solution.py:32
  52.1 0.0 copy-start
  52.1 4.4 %all-to-all-start.1 = ((f32[1536,2,128]{2,1,0:T(2,128)}), f32[1536,2,128]{2,1,0:T(2,128)}, u32[]{:S(2)}, u32[]{:S(2)}) async-start(f32[1536,2,128]{2,1,0:T(2,128)} %copy.70), calls=%async_computation.1 | async-start | bytes 3145728 | tf_op jit(solution)/shard_map/all_to_all | solution.py:46
  56.6 0.0 copy-done
  56.6 0.9 copy.62
  57.5 0.0 copy-start.1
  57.5 0.0 copy-start.3
  57.5 0.0 copy-start.4
  57.5 0.0 copy-start.5
  57.5 1.3 fusion.24
  58.8 3.1 %collective-permute-start = (f32[96,1,2048]{2,0,1:T(8,128)}, f32[96,1,2048]{2,0,1:T(8,128)}, u32[]{:S(2)}, u32[]{:S(2)}) collective-permute-start(f32[96,1,2048]{2,0,1:T(8,128)} %get-tuple-element.9), channel_id=1, source_target_pairs={{0,1},{1,2},{2,3},{3,4},{4,5},{5,6},{6,7},{7,8},{8,9},{9,10},{10,1... | collective-permute-start | bytes 2359304 | tf_op jit(solution)/shard_map/ppermute | solution.py:17
  61.9 1.3 collective-permute-start.1
  63.1 0.0 copy-done.1
  63.2 0.0 copy-done.3
  63.2 0.0 copy-done.4
  63.2 0.0 copy-done.5
  63.2 30.4 %all-to-all-done.1 = f32[1536,2,128]{2,1,0:T(2,128)} async-done(((f32[1536,2,128]{2,1,0:T(2,128)}), f32[1536,2,128]{2,1,0:T(2,128)}, u32[]{:S(2)}, u32[]{:S(2)}) %all-to-all-start.1) | async-done | bytes 1572896 | tf_op jit(solution)/shard_map/all_to_all | solution.py:46
  93.6 2.3 %copy.88 = f32[16,96,2,128]{3,0,1,2:T(8,128)S(1)} copy(f32[16,96,2,128]{3,2,1,0:T(2,128)} %bitcast.4) | data formatting | bytes 3145728 | tf_op jit(solution)/shard_map/all_to_all | solution.py:46
  95.9 0.0 copy-start.2
  95.9 1.4 all_to_all.59
  97.3 0.0 collective-permute-done
  97.3 0.0 collective-permute-done.1
  97.3 0.0 copy-done.2
  97.3 3.8 %fusion.21 = (bf16[96,2,2048]{2,0,1:T(8,128)(2,1)}, f32[96,2,2048]{2,0,1:T(8,128)S(1)}) fusion(f32[96]{0:T(128)S(1)} %get-tuple-element.12, f32[96]{0:T(128)S(1)} %copy-done.2, f32[2,2048]{1,0:T(2,128)S(1)} %convert_element_type.13, f32[96,2,2048]{2,0,1:T(8,128)} %all_to_all.59, f32[96,2,2048]{2,0,1:T(8,128)S(1)} %copy.62, ...), kind=kLoop, calls=%fused_computation.34 | loop fusion | flops 4718592 | bytes 7096000 | tf_op jit(solution)/shard_map/convert_element_type | solution.py:42
  101.1 2.4 %copy.72 = bf16[96,2,2048]{0,1,2:T(2,128)(2,1)S(1)} copy(bf16[96,2,2048]{2,0,1:T(8,128)(2,1)} %get-tuple-element.5) | data formatting | bytes 1572864 | tf_op jit(solution)/shard_map/convert_element_type | solution.py:42
  103.5 32.8 %all_to_all.73 = bf16[96,2,2048]{0,1,2:T(2,128)(2,1)} all-to-all(bf16[96,2,2048]{0,1,2:T(2,128)(2,1)S(1)} %copy.72), channel_id=1, replica_groups=mesh['mode'=16,'cell'=32] {'mode'}, dimensions={2} | all-to-all | bytes 1572864 | tf_op jit(solution)/shard_map/all_to_all | solution.py:44
  136.4 3.6 %copy.82 = bf16[96,2,16,128]{3,0,2,1:T(8,128)(2,1)} copy(bf16[96,2,16,128]{0,1,3,2:T(2,128)(2,1)} %bitcast.37) | data formatting | bytes 1572864 | tf_op jit(solution)/shard_map/all_to_all | solution.py:44
  140.0 4.0 %fusion.4 = f32[1536,2,128]{0,2,1:T(8,128)S(1)} fusion(bf16[1536,2,128]{2,0,1:T(8,128)(2,1)} %bitcast.39, bf16[1536,1536]{1,0:T(8,128)(2,1)} %param.8), kind=kOutput, calls=%fused_computation.4 | convolution fusion | flops 1207959552 | bytes 7077888 | tf_op jit(solution)/shard_map/ij,jkc->ikc/dot_general | solution.py:32
  144.0 2.1 %copy.76 = f32[1536,2,128]{2,1,0:T(2,128)} copy(f32[1536,2,128]{0,2,1:T(8,128)S(1)} %fusion.4) | data formatting | bytes 3145728 | tf_op jit(solution)/shard_map/ij,jkc->ikc/dot_general | solution.py:32
  146.1 3.8 %all-to-all-start.3 = ((f32[1536,2,128]{2,1,0:T(2,128)}), f32[1536,2,128]{2,1,0:T(2,128)S(1)}, u32[]{:S(2)}, u32[]{:S(2)}) async-start(f32[1536,2,128]{2,1,0:T(2,128)} %copy.76), calls=%async_computation.3 | async-start | bytes 3145728 | tf_op jit(solution)/shard_map/all_to_all | solution.py:46
  149.9 1.3 fusion.23
  151.1 3.1 %collective-permute-start.2 = (f32[96,1,2048]{2,0,1:T(8,128)}, f32[96,1,2048]{2,0,1:T(8,128)}, u32[]{:S(2)}, u32[]{:S(2)}) collective-permute-start(f32[96,1,2048]{2,0,1:T(8,128)} %get-tuple-element.7), channel_id=1, source_target_pairs={{0,1},{1,2},{2,3},{3,4},{4,5},{5,6},{6,7},{7,8},{8,9},{9,10},{10,1... | collective-permute-start | bytes 2359304 | tf_op jit(solution)/shard_map/ppermute | solution.py:17
  154.2 1.3 collective-permute-start.3
  155.5 31.9 %all-to-all-done.3 = f32[1536,2,128]{2,1,0:T(2,128)S(1)} async-done(((f32[1536,2,128]{2,1,0:T(2,128)}), f32[1536,2,128]{2,1,0:T(2,128)S(1)}, u32[]{:S(2)}, u32[]{:S(2)}) %all-to-all-start.3) | async-done | bytes 1572896 | tf_op jit(solution)/shard_map/all_to_all | solution.py:46
  187.4 0.1 copy.77
  187.5 0.0 collective-permute-done.2
  187.5 0.0 collective-permute-done.3
  187.6 2.5 %fusion.16 = f32[96,2,2048]{2,0,1:T(8,128)S(1)} fusion(f32[96,2,2048]{2,0,1:T(8,128)S(1)} %get-tuple-element.6, f32[2,16,12,8,128]{4,3,2,1,0:T(8,128)S(1)} %bitcast.35, f32[96,1,2048]{2,0,1:T(8,128)} %collective-permute-done.3, f32[96,1,2048]{2,0,1:T(8,128)} %collective-permute-done.2, f32[96]{0:T(128)S(1)} %get-tuple-element.12, f32[96]{0:T(128)S(1)} %copy-done.2, ...), kind=kLoop, calls=%fused_computation.20 | loop fusion | flops 4325376 | bytes 6309568 | tf_op jit(solution)/shard_map/div | solution.py:50
  190.0 2.4 %copy.79 = f32[96,2,2048]{2,1,0:T(2,128)} copy(f32[96,2,2048]{2,0,1:T(8,128)S(1)} %fusion.16) | data formatting | bytes 3145728 | tf_op jit(solution)/shard_map/div | solution.py:50
  (3 shorter events, 0.0 us)
Async XLA Ops:
  52.1 4.5 %copy-start = (f32[96,2,2048]{2,1,0:T(2,128)S(1)}, f32[96,2,2048]{2,1,0:T(2,128)}, u32[]{:S(2)}) copy-start(f32[96,2,2048]{2,1,0:T(2,128)} %param.7) | copy-start | bytes 4718596
  52.1 41.5 %all-to-all-start.1 = ((f32[1536,2,128]{2,1,0:T(2,128)}), f32[1536,2,128]{2,1,0:T(2,128)}, u32[]{:S(2)}, u32[]{:S(2)}) async-start(f32[1536,2,128]{2,1,0:T(2,128)} %copy.70), calls=%async_computation.1 | async-start | bytes 3145728 | tf_op jit(solution)/shard_map/all_to_all | solution.py:46
  57.5 5.7 %copy-start.1 = (s32[2,2048]{1,0:T(2,128)S(1)}, s32[2,2048]{1,0:T(2,128)}, u32[]{:S(2)}) copy-start(s32[2,2048]{1,0:T(2,128)} %param.13) | copy-start | bytes 49156
  57.5 5.7 %copy-start.3 = (f32[96]{0:T(128)S(1)}, f32[96]{0:T(128)}, u32[]{:S(2)}) copy-start(f32[96]{0:T(128)} %param.9) | copy-start | bytes 1156
  57.5 5.7 %copy-start.4 = (f32[96]{0:T(128)S(1)}, f32[96]{0:T(128)}, u32[]{:S(2)}) copy-start(f32[96]{0:T(128)} %param.10) | copy-start | bytes 1156
  57.5 5.7 %copy-start.5 = (f32[96]{0:T(128)S(1)}, f32[96]{0:T(128)}, u32[]{:S(2)}) copy-start(f32[96]{0:T(128)} %param.11) | copy-start | bytes 1156
  58.8 38.5 %collective-permute-start = (f32[96,1,2048]{2,0,1:T(8,128)}, f32[96,1,2048]{2,0,1:T(8,128)}, u32[]{:S(2)}, u32[]{:S(2)}) collective-permute-start(f32[96,1,2048]{2,0,1:T(8,128)} %get-tuple-element.9), channel_id=1, source_target_pairs={{0,1},{1,2},{2,3},{3,4},{4,5},{5,6},{6,7},{7,8},{8,9},{9,10},{10,1... | collective-permute-start | bytes 2359304 | tf_op jit(solution)/shard_map/ppermute | solution.py:17
  61.9 35.5 %collective-permute-start.1 = (f32[96,1,2048]{2,0,1:T(8,128)}, f32[96,1,2048]{2,0,1:T(8,128)}, u32[]{:S(2)}, u32[]{:S(2)}) collective-permute-start(f32[96,1,2048]{2,0,1:T(8,128)} %get-tuple-element.10), channel_id=1, source_target_pairs={{1,0},{2,1},{3,2},{4,3},{5,4},{6,5},{7,6},{8,7},{9,8},{10,9},{11,1... | collective-permute-start | bytes 2359304 | tf_op jit(solution)/shard_map/ppermute | solution.py:19
  95.9 1.4 copy-start.2
  146.1 41.4 %all-to-all-start.3 = ((f32[1536,2,128]{2,1,0:T(2,128)}), f32[1536,2,128]{2,1,0:T(2,128)S(1)}, u32[]{:S(2)}, u32[]{:S(2)}) async-start(f32[1536,2,128]{2,1,0:T(2,128)} %copy.76), calls=%async_computation.3 | async-start | bytes 3145728 | tf_op jit(solution)/shard_map/all_to_all | solution.py:46
  151.1 36.4 %collective-permute-start.2 = (f32[96,1,2048]{2,0,1:T(8,128)}, f32[96,1,2048]{2,0,1:T(8,128)}, u32[]{:S(2)}, u32[]{:S(2)}) collective-permute-start(f32[96,1,2048]{2,0,1:T(8,128)} %get-tuple-element.7), channel_id=1, source_target_pairs={{0,1},{1,2},{2,3},{3,4},{4,5},{5,6},{6,7},{7,8},{8,9},{9,10},{10,1... | collective-permute-start | bytes 2359304 | tf_op jit(solution)/shard_map/ppermute | solution.py:17
  154.2 33.3 %collective-permute-start.3 = (f32[96,1,2048]{2,0,1:T(8,128)}, f32[96,1,2048]{2,0,1:T(8,128)}, u32[]{:S(2)}, u32[]{:S(2)}) collective-permute-start(f32[96,1,2048]{2,0,1:T(8,128)} %get-tuple-element.8), channel_id=1, source_target_pairs={{1,0},{2,1},{3,2},{4,3},{5,4},{6,5},{7,6},{8,7},{9,8},{10,9},{11,1... | collective-permute-start | bytes 2359304 | tf_op jit(solution)/shard_map/ppermute | solution.py:19
where the time goes:
time: 193 us; the launch traced here: 192 us
  blocking collectives  70.7 us (37%)
  waiting for transfers between devices  62.3 us (32%)
  local copies, waits for them, and re-layouts  28.1 us (15%)
  starting transfers between devices  16.9 us (9%)
  matrix products  7.76 us (4%)
  other arithmetic  6.28 us (3%)
    all_to_all x2, blocking collectives, shards(): lax.all_to_all(narrow, 'mode', split_axis=2, concat_axis=0, tiled=True)  70.7 us
    all_to_all x2, waiting for transfers between devices, shards(): lax.all_to_all(complete, 'mode', split_axis=0, concat_axis=2, tiled=True)  62.3 us
    dot_general x2, local copies, waits for them, and re-layouts, apply_matrix(): jnp.einsum('ij,jkc->ikc', scatter_matrix, block, preferred_element_type=j...  8.66 us
    all_to_all x2, starting transfers between devices, shards(): lax.all_to_all(complete, 'mode', split_axis=0, concat_axis=2, tiled=True)  8.22 us
    dot_general x2, matrix products, apply_matrix(): jnp.einsum('ij,jkc->ikc', scatter_matrix, block, preferred_element_type=j...  7.76 us
    ppermute x2, starting transfers between devices, padded_2(): lax.ppermute(tail, axis, [(i, (i + 1) % count) for i in range(ends)])  6.14 us
    all_to_all x2, local copies, waits for them, and re-layouts, shards(): lax.all_to_all(narrow, 'mode', split_axis=2, concat_axis=0, tiled=True)  4.4 us
  transfers between devices with their start and end apart: 6, of which 2 were waited for; matrix products, arithmetic and copies ran while one was open for 3% of the time, Pallas kernels for 0%

commit v1 on v0

v1 whole, which is shorter than its diff:
```python
import jax
import jax.numpy as jnp
from jax import lax
from jax.sharding import PartitionSpec as P

F32 = jnp.float32
BF16 = jnp.bfloat16


def shift_pairs(count, step):
    return [(i, i + step) for i in range(count) if 0 <= i + step < count]


def swap(values, axis):
    onward, back = values
    count = lax.axis_size(axis)
    return (
        lax.ppermute(onward, axis, shift_pairs(count, 1)),
        lax.ppermute(back, axis, shift_pairs(count, -1)),
    )


def shards(initial, scatter_matrix, speed_x, speed_y, relaxation, emission, heater):
    modes, cols, length = initial.shape
    groups = lax.axis_size("mode")
    span = length // groups
    cells = cols * span
    total = modes * groups

    packed = initial.astype(BF16).reshape(modes, cols, groups, span)
    packed = packed.transpose(2, 0, 1, 3).reshape(groups, modes, cells)
    own = lax.all_to_all(packed, "mode", 0, 0, tiled=True).reshape(total, cells)

    params = lax.all_gather(
        jnp.stack([speed_x, speed_y, relaxation, emission]), "mode", axis=1, tiled=True
    )
    sx, sy, rel, emit = (params[k][:, None] for k in range(4))
    inverse = 1.0 / (rel + jnp.abs(sx) + jnp.abs(sy))
    x_up, x_down = jnp.maximum(sx, 0.0) * inverse, jnp.maximum(-sx, 0.0) * inverse
    y_up, y_down = jnp.maximum(sy, 0.0) * inverse, jnp.maximum(-sy, 0.0) * inverse
    heat = lax.dynamic_slice_in_dim(heater, lax.axis_index("mode") * span, span, axis=1)
    source = heat.astype(F32).reshape(1, cells) * (emit * inverse)

    def ends(field):
        first = jnp.concatenate([field[:, c * span : c * span + 1] for c in range(cols)], axis=1)
        last = jnp.concatenate([field[:, (c + 1) * span - 1 : (c + 1) * span] for c in range(cols)], axis=1)
        return first.T, last.T

    def along_y(field, before, after):
        before, after = before.T, after.T
        up, down = [], []
        for c in range(cols):
            part = field[:, c * span : (c + 1) * span]
            up += [before[:, c : c + 1], part[:, :-1]]
            down += [part[:, 1:], after[:, c : c + 1]]
        return (
            y_up * jnp.concatenate(up, axis=1).astype(F32)
            + y_down * jnp.concatenate(down, axis=1).astype(F32)
        )

    def scatter(field):
        return inverse * jnp.dot(scatter_matrix, field, preferred_element_type=F32)

    def inner_x(field):
        zero = jnp.zeros((total, span), F32)
        wide = field.astype(F32)
        return x_up * jnp.concatenate([zero, wide[:, :-span]], axis=1) + x_down * jnp.concatenate(
            [wide[:, span:], zero], axis=1
        )

    def outer_x(left, right):
        zero = jnp.zeros((total, cells - 2 * span), F32)
        return jnp.concatenate(
            [x_up * left.astype(F32), zero, x_down * right.astype(F32)], axis=1
        )

    x_before, x_after = swap((own[:, -span:], own[:, :span]), "cell")
    first, last = ends(own)
    y_before, y_after = swap((last, first), "mode")
    partial = scatter(own) + source + inner_x(own) + along_y(own, y_before, y_after)
    sent = partial.astype(BF16)
    x_before_2, x_after_2 = swap((sent[:, -span:], sent[:, :span]), "cell")
    field = (partial + outer_x(x_before, x_after)).astype(BF16)

    first, last = ends(field)
    y_before, y_after = swap((last, first), "mode")
    result = (
        scatter(field)
        + source
        + inner_x(field)
        + along_y(field, y_before, y_after)
        + outer_x(x_before_2, x_after_2)
    )
    result = result.astype(BF16).reshape(groups, modes, cells)
    out = lax.all_to_all(result, "mode", 0, 0, tiled=True)
    out = out.reshape(groups, modes, cols, span).transpose(1, 2, 0, 3)
    return out.reshape(modes, cols, length).astype(F32)


def solution(mesh):
    return jax.shard_map(
        shards,
        mesh=mesh,
        in_specs=(
            P("mode", "cell", None),
            P(),
            P("mode"),
            P("mode"),
            P("mode"),
            P("mode"),
            P("cell", None),
        ),
        out_specs=P("mode", "cell", None),
        check_vma=False,
    )
```

time: 193 us -> 133 us (0.69)
  the two profiles are of different devices: /device:TPU:1 before, /device:TPU:199 now
where the time goes in v1:
time: 133 us
  blocking collectives  60.8 us (46%)
  starting transfers between devices  29.6 us (22%)
  waiting for transfers between devices  25.7 us (19%)
  matrix products  7 us (5%)
  local copies, waits for them, and re-layouts  5.79 us (4%)
  other arithmetic  3.41 us (3%)
    all_gather x1, blocking collectives, shards(): lax.all_gather(jnp.stack([speed_x, speed_y, relaxation, emission]), 'mode...  31.1 us
    all_to_all x1, blocking collectives, shards(): out = lax.all_to_all(result, 'mode', 0, 0, tiled=True)  29.7 us
    ppermute x4, waiting for transfers between devices, swap(): lax.ppermute(onward, axis, shift_pairs(count, 1))  13.5 us
    ppermute x4, starting transfers between devices, swap(): lax.ppermute(onward, axis, shift_pairs(count, 1))  12.2 us
    ppermute x4, waiting for transfers between devices, swap(): lax.ppermute(back, axis, shift_pairs(count, -1))  12.2 us
    ppermute x4, starting transfers between devices, swap(): lax.ppermute(back, axis, shift_pairs(count, -1))  9.61 us
    all_to_all x1, starting transfers between devices, shards(): own = lax.all_to_all(packed, 'mode', 0, 0, tiled=True).reshape(total, cells)  7.79 us
    dot_general x2, matrix products, scatter(): return inverse * jnp.dot(scatter_matrix, field, preferred_element_type=F32)  7 us
  transfers between devices with their start and end apart: 9, of which 4 were waited for; matrix products, arithmetic and copies ran while one was open for 1% of the time, Pallas kernels for 0%

profile of v1, /device:TPU:199, one launch (start us, length us, event | category | flops | bytes accessed | tf_op | source)
XLA Modules:
  0.0 132.8 jit_solution(13150188572632507476)
XLA Ops:
  0.0 2.2 %bitcast_bitcast_fusion = bf16[16,96,2,128]{3,2,1,0:T(2,128)(2,1)S(1)} fusion(f32[96,2,2048]{2,1,0:T(2,128)} %param.7), kind=kLoop, calls=%fused_computation.14 | loop fusion | flops 393216 | bytes 2359296 | tf_op jit(solution)/shard_map/transpose | solution.py:31
  2.2 0.0 copy-start
  2.2 0.0 copy-start.1
  2.2 0.0 copy-start.2
  2.3 0.0 copy-start.3
  2.3 1.4 %reshape.154 = bf16[16,96,256]{2,1,0:T(8,128)(2,1)} reshape(bf16[16,96,2,128]{3,2,1,0:T(2,128)(2,1)S(1)} %bitcast_bitcast_fusion) | data formatting | bytes 1572864 | tf_op jit(solution)/shard_map/reshape | solution.py:31
  3.6 7.8 %all-to-all-start = ((bf16[16,96,256]{2,1,0:T(8,128)(2,1)}), bf16[16,96,256]{2,1,0:T(8,128)(2,1)S(1)}, u32[]{:S(2)}, u32[]{:S(2)}) async-start(bf16[16,96,256]{2,1,0:T(8,128)(2,1)} %reshape.154), calls=%async_computation | async-start | bytes 1572864 | tf_op jit(solution)/shard_map/all_to_all | solution.py:32
  11.4 0.0 copy-done
  11.5 31.1 %all-gather = f32[16,96,4]{1,2,0:T(4,128)S(1)} all-gather(f32[1,96,4]{1,2,0:T(4,128)S(1)} %maximum_bitcast_fusion.4), channel_id=1, replica_groups=mesh['mode'=16,'cell'=32] {'mode'}, dimensions={0}, use_global_device_ids=true | all-gather | bytes 26112 | tf_op jit(solution)/shard_map/all_gather | solution.py:34
  42.6 0.1 reshape.160
  42.7 0.7 convert_bitcast_fusion.1
  43.4 0.1 slice_reduce_fusion
  43.5 0.0 all-to-all-done
  43.5 0.3 copy.27
  43.8 0.1 fusion.13
  43.9 0.2 fusion.15
  44.1 0.2 fusion.17
  44.3 1.9 %collective-permute-start = (bf16[2,1536]{1,0:T(2,128)(2,1)S(1)}, bf16[2,1536]{1,0:T(2,128)(2,1)S(1)}, u32[]{:S(2)}, u32[]{:S(2)}) collective-permute-start(bf16[2,1536]{1,0:T(2,128)(2,1)S(1)} %maximum_bitcast_fusion), channel_id=1, source_target_pairs={{0,32},{32,64},{64,96},{96,128},{128,160},{160,192},{192,224},{224... | collective-permute-start | bytes 18440 | tf_op jit(solution)/shard_map/ppermute | solution.py:18
  46.3 2.4 %collective-permute-start.1 = (bf16[2,1536]{1,0:T(2,128)(2,1)S(1)}, bf16[2,1536]{1,0:T(2,128)(2,1)S(1)}, u32[]{:S(2)}, u32[]{:S(2)}) collective-permute-start(bf16[2,1536]{1,0:T(2,128)(2,1)S(1)} %maximum_bitcast_fusion.1), channel_id=1, source_target_pairs={{32,0},{64,32},{96,64},{128,96},{160,128},{192,160},{224,192},{256... | collective-permute-start | bytes 18440 | tf_op jit(solution)/shard_map/ppermute | solution.py:19
  48.7 5.1 %collective-permute-start.2 = (bf16[1536,128]{0,1:T(8,128)(2,1)S(1)}, bf16[1536,128]{0,1:T(8,128)(2,1)S(1)}, u32[]{:S(2)}, u32[]{:S(2)}) collective-permute-start(bf16[1536,128]{0,1:T(8,128)(2,1)S(1)} %get-tuple-element.23), channel_id=1, source_target_pairs={{0,1},{1,2},{2,3},{3,4},{4,5},{5,6},{6,7},{7,8},{8,9},{9,10},{10,1... | collective-permute-start | bytes 1179656 | tf_op jit(solution)/shard_map/ppermute | solution.py:18
  53.8 1.9 %collective-permute-start.3 = (bf16[1536,128]{0,1:T(8,128)(2,1)S(1)}, bf16[1536,128]{0,1:T(8,128)(2,1)S(1)}, u32[]{:S(2)}, u32[]{:S(2)}) collective-permute-start(bf16[1536,128]{0,1:T(8,128)(2,1)S(1)} %get-tuple-element.24), channel_id=1, source_target_pairs={{1,0},{2,1},{3,2},{4,3},{5,4},{6,5},{7,6},{8,7},{9,8},{10,9},{11,1... | collective-permute-start | bytes 1179656 | tf_op jit(solution)/shard_map/ppermute | solution.py:19
  55.7 0.0 collective-permute-done
  55.8 0.0 collective-permute-done.1
  55.8 6.8 %collective-permute-done.2 = bf16[1536,128]{0,1:T(8,128)(2,1)S(1)} collective-permute-done((bf16[1536,128]{0,1:T(8,128)(2,1)S(1)}, bf16[1536,128]{0,1:T(8,128)(2,1)S(1)}, u32[]{:S(2)}, u32[]{:S(2)}) %collective-permute-start.2) | collective-permute-done | bytes 393248 | tf_op jit(solution)/shard_map/ppermute | solution.py:18
  62.6 0.1 convert_multiply_fusion.3
  62.7 7.3 %collective-permute-done.3 = bf16[1536,128]{0,1:T(8,128)(2,1)S(1)} collective-permute-done((bf16[1536,128]{0,1:T(8,128)(2,1)S(1)}, bf16[1536,128]{0,1:T(8,128)(2,1)S(1)}, u32[]{:S(2)}, u32[]{:S(2)}) %collective-permute-start.3) | collective-permute-done | bytes 393248 | tf_op jit(solution)/shard_map/ppermute | solution.py:19
  70.0 0.1 convert_multiply_fusion.2
  70.1 0.0 slice-start
  70.1 0.0 slice-start.1
  70.1 4.7 %fusion.7 = (bf16[1536,256]{0,1:T(8,128)(2,1)S(1)}, bf16[1536,256]{0,1:T(8,128)(2,1)S(1)}) fusion(f32[1536,128]{0,1:T(8,128)S(1)} %convert_multiply_fusion.2, f32[1536,128]{0,1:T(8,128)S(1)} %convert_multiply_fusion.3, bf16[1536,1]{0,1:T(2,128)(2,1)S(1)} %get-tuple-element.47, bf16[1536,127]{0,1:T(8,128)(2,1)S(1)} %get-tuple-element.28, ...), kind=kOutput, calls=%fused_computation.11 | convolution fusion | flops 1220149248 | bytes 11834368 | tf_op jit(solution)/shard_map/dot_general | solution.py:62
  74.9 0.2 fusion.10
  75.1 0.2 fusion.12
  75.3 0.1 fusion.14
  75.3 3.2 %collective-permute-start.4 = (bf16[2,1536]{1,0:T(2,128)(2,1)S(1)}, bf16[2,1536]{1,0:T(2,128)(2,1)S(1)}, u32[]{:S(2)}, u32[]{:S(2)}) collective-permute-start(bf16[2,1536]{1,0:T(2,128)(2,1)S(1)} %maximum_bitcast_fusion.2), channel_id=1, source_target_pairs={{0,32},{32,64},{64,96},{96,128},{128,160},{160,192},{192,224},{224... | collective-permute-start | bytes 18440 | tf_op jit(solution)/shard_map/ppermute | solution.py:18
  78.6 1.9 %collective-permute-start.5 = (bf16[2,1536]{1,0:T(2,128)(2,1)S(1)}, bf16[2,1536]{1,0:T(2,128)(2,1)S(1)}, u32[]{:S(2)}, u32[]{:S(2)}) collective-permute-start(bf16[2,1536]{1,0:T(2,128)(2,1)S(1)} %maximum_bitcast_fusion.3), channel_id=1, source_target_pairs={{32,0},{64,32},{96,64},{128,96},{160,128},{192,160},{224,192},{256... | collective-permute-start | bytes 18440 | tf_op jit(solution)/shard_map/ppermute | solution.py:19
  80.5 1.9 %collective-permute-start.6 = (bf16[1536,128]{0,1:T(8,128)(2,1)S(1)}, bf16[1536,128]{0,1:T(8,128)(2,1)S(1)}, u32[]{:S(2)}, u32[]{:S(2)}) collective-permute-start(bf16[1536,128]{0,1:T(8,128)(2,1)S(1)} %get-tuple-element.25), channel_id=1, source_target_pairs={{0,1},{1,2},{2,3},{3,4},{4,5},{5,6},{6,7},{7,8},{8,9},{9,10},{10,1... | collective-permute-start | bytes 1179656 | tf_op jit(solution)/shard_map/ppermute | solution.py:18
  82.5 3.4 %collective-permute-start.7 = (bf16[1536,128]{0,1:T(8,128)(2,1)S(1)}, bf16[1536,128]{0,1:T(8,128)(2,1)S(1)}, u32[]{:S(2)}, u32[]{:S(2)}) collective-permute-start(bf16[1536,128]{0,1:T(8,128)(2,1)S(1)} %get-tuple-element.26), channel_id=1, source_target_pairs={{1,0},{2,1},{3,2},{4,3},{5,4},{6,5},{7,6},{8,7},{9,8},{10,9},{11,1... | collective-permute-start | bytes 1179656 | tf_op jit(solution)/shard_map/ppermute | solution.py:19
  85.8 0.0 collective-permute-done.4
  85.9 0.0 collective-permute-done.5
  85.9 6.7 %collective-permute-done.6 = bf16[1536,128]{0,1:T(8,128)(2,1)S(1)} collective-permute-done((bf16[1536,128]{0,1:T(8,128)(2,1)S(1)}, bf16[1536,128]{0,1:T(8,128)(2,1)S(1)}, u32[]{:S(2)}, u32[]{:S(2)}) %collective-permute-start.6) | collective-permute-done | bytes 393248 | tf_op jit(solution)/shard_map/ppermute | solution.py:18
  92.6 0.1 convert_multiply_fusion.1
  92.7 4.9 %collective-permute-done.7 = bf16[1536,128]{0,1:T(8,128)(2,1)S(1)} collective-permute-done((bf16[1536,128]{0,1:T(8,128)(2,1)S(1)}, bf16[1536,128]{0,1:T(8,128)(2,1)S(1)}, u32[]{:S(2)}, u32[]{:S(2)}) %collective-permute-start.7) | collective-permute-done | bytes 393248 | tf_op jit(solution)/shard_map/ppermute | solution.py:19
  97.5 0.1 convert_multiply_fusion
  97.6 2.3 %fusion.8 = bf16[1536,256]{0,1:T(8,128)(2,1)S(1)} fusion(f32[1536,128]{0,1:T(8,128)S(1)} %convert_multiply_fusion, f32[1536,128]{0,1:T(8,128)S(1)} %convert_multiply_fusion.1, bf16[1536,256]{0,1:T(8,128)(2,1)S(1)} %get-tuple-element.11, bf16[1536,1536]{1,0:T(8,128)(2,1)S(1)} %bitcast.67, f32[1536,128]{0,1:T(8,128)S(1)} %get-tuple-element.22, ...), kind=kOutput, calls=%fused_computation.13 | convolution fusion | flops 1219756032 | bytes 11047936 | tf_op jit(solution)/shard_map/dot_general | solution.py:62
  100.0 0.3 copy.38
  100.2 29.7 %all_to_all.10 = bf16[16,96,256]{2,1,0:T(8,128)(2,1)S(1)} all-to-all(bf16[16,96,256]{2,1,0:T(8,128)(2,1)S(1)} %bitcast.56), channel_id=1, replica_groups=mesh['mode'=16,'cell'=32] {'mode'}, dimensions={0} | all-to-all | bytes 1572864 | tf_op jit(solution)/shard_map/all_to_all | solution.py:95
  130.0 0.8 reshape.158
  130.7 2.0 %copy_bitcast_fusion = f32[96,2,2048]{2,1,0:T(2,128)} fusion(f32[16,96,2,128]{3,2,1,0:T(2,128)S(1)} %reshape.158), kind=kLoop, calls=%fused_computation.9 | loop fusion | bytes 3145728 | tf_op jit(solution)/shard_map/convert_element_type | solution.py:97
  (19 shorter events, 0.2 us)
Async XLA Ops:
  2.2 9.2 %copy-start = (f32[96]{0:T(128)S(1)}, f32[96]{0:T(128)}, u32[]{:S(2)}) copy-start(f32[96]{0:T(128)} %param.12) | copy-start | bytes 1156
  2.2 9.2 %copy-start.1 = (f32[96]{0:T(128)S(1)}, f32[96]{0:T(128)}, u32[]{:S(2)}) copy-start(f32[96]{0:T(128)} %param.11) | copy-start | bytes 1156
  2.2 9.2 %copy-start.2 = (f32[96]{0:T(128)S(1)}, f32[96]{0:T(128)}, u32[]{:S(2)}) copy-start(f32[96]{0:T(128)} %param.10) | copy-start | bytes 1156
  2.3 9.2 %copy-start.3 = (f32[96]{0:T(128)S(1)}, f32[96]{0:T(128)}, u32[]{:S(2)}) copy-start(f32[96]{0:T(128)} %param.9) | copy-start | bytes 1156
  3.6 39.9 %all-to-all-start = ((bf16[16,96,256]{2,1,0:T(8,128)(2,1)}), bf16[16,96,256]{2,1,0:T(8,128)(2,1)S(1)}, u32[]{:S(2)}, u32[]{:S(2)}) async-start(bf16[16,96,256]{2,1,0:T(8,128)(2,1)} %reshape.154), calls=%async_computation | async-start | bytes 1572864 | tf_op jit(solution)/shard_map/all_to_all | solution.py:32
  44.3 11.4 %collective-permute-start = (bf16[2,1536]{1,0:T(2,128)(2,1)S(1)}, bf16[2,1536]{1,0:T(2,128)(2,1)S(1)}, u32[]{:S(2)}, u32[]{:S(2)}) collective-permute-start(bf16[2,1536]{1,0:T(2,128)(2,1)S(1)} %maximum_bitcast_fusion), channel_id=1, source_target_pairs={{0,32},{32,64},{64,96},{96,128},{128,160},{160,192},{192,224},{224... | collective-permute-start | bytes 18440 | tf_op jit(solution)/shard_map/ppermute | solution.py:18
  46.3 9.5 %collective-permute-start.1 = (bf16[2,1536]{1,0:T(2,128)(2,1)S(1)}, bf16[2,1536]{1,0:T(2,128)(2,1)S(1)}, u32[]{:S(2)}, u32[]{:S(2)}) collective-permute-start(bf16[2,1536]{1,0:T(2,128)(2,1)S(1)} %maximum_bitcast_fusion.1), channel_id=1, source_target_pairs={{32,0},{64,32},{96,64},{128,96},{160,128},{192,160},{224,192},{256... | collective-permute-start | bytes 18440 | tf_op jit(solution)/shard_map/ppermute | solution.py:19
  48.7 14.0 %collective-permute-start.2 = (bf16[1536,128]{0,1:T(8,128)(2,1)S(1)}, bf16[1536,128]{0,1:T(8,128)(2,1)S(1)}, u32[]{:S(2)}, u32[]{:S(2)}) collective-permute-start(bf16[1536,128]{0,1:T(8,128)(2,1)S(1)} %get-tuple-element.23), channel_id=1, source_target_pairs={{0,1},{1,2},{2,3},{3,4},{4,5},{5,6},{6,7},{7,8},{8,9},{9,10},{10,1... | collective-permute-start | bytes 1179656 | tf_op jit(solution)/shard_map/ppermute | solution.py:18
  53.8 16.2 %collective-permute-start.3 = (bf16[1536,128]{0,1:T(8,128)(2,1)S(1)}, bf16[1536,128]{0,1:T(8,128)(2,1)S(1)}, u32[]{:S(2)}, u32[]{:S(2)}) collective-permute-start(bf16[1536,128]{0,1:T(8,128)(2,1)S(1)} %get-tuple-element.24), channel_id=1, source_target_pairs={{1,0},{2,1},{3,2},{4,3},{5,4},{6,5},{7,6},{8,7},{9,8},{10,9},{11,1... | collective-permute-start | bytes 1179656 | tf_op jit(solution)/shard_map/ppermute | solution.py:19
  70.1 27.5 %slice-start = ((s8[4718592]{0:T(1024)(128)(4,1)}), s8[4194304]{0:T(1024)(128)(4,1)S(1)}, s32[]{:S(2)}) async-start(s8[4718592]{0:T(1024)(128)(4,1)} %bitcast.66), calls=%async_computation.2 | async-start | bytes 8388608
  70.1 27.5 %slice-start.1 = ((s8[4718592]{0:T(1024)(128)(4,1)}), s8[524288]{0:T(1024)(128)(4,1)S(1)}, s32[]{:S(2)}) async-start(s8[4718592]{0:T(1024)(128)(4,1)} %bitcast.66), calls=%async_computation.3 | async-start | bytes 1048576
  75.3 10.5 %collective-permute-start.4 = (bf16[2,1536]{1,0:T(2,128)(2,1)S(1)}, bf16[2,1536]{1,0:T(2,128)(2,1)S(1)}, u32[]{:S(2)}, u32[]{:S(2)}) collective-permute-start(bf16[2,1536]{1,0:T(2,128)(2,1)S(1)} %maximum_bitcast_fusion.2), channel_id=1, source_target_pairs={{0,32},{32,64},{64,96},{96,128},{128,160},{160,192},{192,224},{224... | collective-permute-start | bytes 18440 | tf_op jit(solution)/shard_map/ppermute | solution.py:18
  78.6 7.3 %collective-permute-start.5 = (bf16[2,1536]{1,0:T(2,128)(2,1)S(1)}, bf16[2,1536]{1,0:T(2,128)(2,1)S(1)}, u32[]{:S(2)}, u32[]{:S(2)}) collective-permute-start(bf16[2,1536]{1,0:T(2,128)(2,1)S(1)} %maximum_bitcast_fusion.3), channel_id=1, source_target_pairs={{32,0},{64,32},{96,64},{128,96},{160,128},{192,160},{224,192},{256... | collective-permute-start | bytes 18440 | tf_op jit(solution)/shard_map/ppermute | solution.py:19
  80.5 12.0 %collective-permute-start.6 = (bf16[1536,128]{0,1:T(8,128)(2,1)S(1)}, bf16[1536,128]{0,1:T(8,128)(2,1)S(1)}, u32[]{:S(2)}, u32[]{:S(2)}) collective-permute-start(bf16[1536,128]{0,1:T(8,128)(2,1)S(1)} %get-tuple-element.25), channel_id=1, source_target_pairs={{0,1},{1,2},{2,3},{3,4},{4,5},{5,6},{6,7},{7,8},{8,9},{9,10},{10,1... | collective-permute-start | bytes 1179656 | tf_op jit(solution)/shard_map/ppermute | solution.py:18
  82.5 15.1 %collective-permute-start.7 = (bf16[1536,128]{0,1:T(8,128)(2,1)S(1)}, bf16[1536,128]{0,1:T(8,128)(2,1)S(1)}, u32[]{:S(2)}, u32[]{:S(2)}) collective-permute-start(bf16[1536,128]{0,1:T(8,128)(2,1)S(1)} %get-tuple-element.26), channel_id=1, source_target_pairs={{1,0},{2,1},{3,2},{4,3},{5,4},{6,5},{7,6},{8,7},{9,8},{10,9},{11,1... | collective-permute-start | bytes 1179656 | tf_op jit(solution)/shard_map/ppermute | solution.py:19

commit v2 on v0

v2 whole, which is shorter than its diff:
```python
import jax
import jax.numpy as jnp
from jax import lax
from jax.sharding import PartitionSpec as P

F32 = jnp.float32
BF16 = jnp.bfloat16
LANES = 128


def shift_pairs(count, step):
    return [(i, i + step) for i in range(count) if 0 <= i + step < count]


def swap(onward, back):
    count = lax.axis_size("cell")
    return (
        lax.ppermute(onward, "cell", shift_pairs(count, 1)),
        lax.ppermute(back, "cell", shift_pairs(count, -1)),
    )


def two_parts(vectors):
    high = lax.reduce_precision(vectors, 8, 7)
    return high.astype(BF16), (vectors - high).astype(BF16)


def shards(initial, scatter_matrix, speed_x, speed_y, relaxation, emission, heater):
    modes, cols, length = initial.shape
    groups = lax.axis_size("mode")
    span = length // groups
    cells = cols * span
    total = modes * groups

    packed = initial.astype(BF16).reshape(modes, cols, groups, span).transpose(2, 0, 1, 3)
    low = jnp.pad(packed[:-1, :, :, span - 2 :], ((1, 0), (0, 0), (0, 0), (0, 0)))
    high = jnp.pad(packed[1:, :, :, :2], ((0, 1), (0, 0), (0, 0), (0, 0)))
    edges = jnp.concatenate([low, high], axis=3).transpose(0, 2, 3, 1)
    edges = edges.reshape(groups, 4 * cols, modes)
    inverse = 1.0 / (relaxation + jnp.abs(speed_x) + jnp.abs(speed_y))
    vectors = jnp.stack([speed_x * inverse, speed_y * inverse, inverse, emission * inverse])
    vectors = jnp.concatenate(two_parts(vectors), axis=0)
    vectors = jnp.broadcast_to(vectors[None], (groups, 8, modes))
    extra = jnp.concatenate([edges, vectors], axis=1)
    extra = jnp.pad(extra, ((0, 0), (0, 0), (0, LANES - modes))).reshape(groups, 8, 2 * LANES)
    packed = packed.reshape(groups, modes, cells)
    received = lax.all_to_all(
        jnp.concatenate([packed, extra], axis=1), "mode", 0, 0, tiled=True
    )

    own = received[:, :modes].reshape(total, cols, span).transpose(1, 2, 0)
    extra = received[:, modes:].reshape(groups, 16, LANES)[:, :, :modes]
    extra = extra.transpose(1, 0, 2).reshape(16, total)
    edges = extra[:8].reshape(cols, 4, total)
    own = jnp.concatenate([edges[:, :2], own, edges[:, 2:]], axis=1)
    vectors = extra[8:12].astype(F32) + extra[12:].astype(F32)
    x_up, x_down = jnp.maximum(vectors[0], 0.0), jnp.maximum(-vectors[0], 0.0)
    y_up, y_down = jnp.maximum(vectors[1], 0.0), jnp.maximum(-vectors[1], 0.0)
    inverse, emit = vectors[2], vectors[3]
    heat = jnp.pad(heater.astype(F32), ((0, 0), (1, 1)))
    heat = lax.dynamic_slice_in_dim(heat, lax.axis_index("mode") * span, span + 2, axis=1)
    heat = heat[:, :, None]

    def scatter(field):
        return inverse * lax.dot_general(
            field, scatter_matrix, (((2,), (1,)), ((), ())), preferred_element_type=F32
        )

    def local(scattered, field, heat):
        wide = field.astype(F32)
        inner = wide[:, 1:-1]
        first = x_down * inner[1]
        second = x_up * inner[0]
        return (
            scattered
            + heat * emit
            + y_up * wide[:, :-2]
            + y_down * wide[:, 2:]
            + jnp.stack([first, second])
        )

    left, right = swap(own[1, 1:-1], own[0, 1:-1])
    partial = local(scatter(own[:, 1:-1]), own, heat)
    partial = lax.optimization_barrier(partial)
    sent = partial[:, 1:-1].astype(BF16)
    left_2, right_2 = swap(sent[1], sent[0])
    field = partial + jnp.stack([x_up * left.astype(F32), x_down * right.astype(F32)])

    result = local(scatter(field[:, 1:-1].astype(BF16)), field, heat[:, 1:-1])
    result = lax.optimization_barrier(result)
    result = result + jnp.stack([x_up * left_2.astype(F32), x_down * right_2.astype(F32)])
    result = result.astype(BF16).transpose(2, 0, 1).reshape(groups, modes, cells)
    out = lax.all_to_all(result, "mode", 0, 0, tiled=True)
    out = out.reshape(groups, modes, cols, span).transpose(1, 2, 0, 3)
    return out.reshape(modes, cols, length).astype(F32)


def solution(mesh):
    return jax.shard_map(
        shards,
        mesh=mesh,
        in_specs=(
            P("mode", "cell", None),
            P(),
            P("mode"),
            P("mode"),
            P("mode"),
            P("mode"),
            P("cell", None),
        ),
        out_specs=P("mode", "cell", None),
        check_vma=False,
    )
```

time: 193 us -> 116 us (0.60)
  the two profiles are of different devices: /device:TPU:1 before, /device:TPU:257 now
where the time goes in v2:
time: 116 us
  waiting for transfers between devices  49.6 us (43%)
  blocking collectives  26.6 us (23%)
  starting transfers between devices  18.6 us (16%)
  local copies, waits for them, and re-layouts  9.92 us (9%)
  matrix products  5.7 us (5%)
  other arithmetic  4.9 us (4%)
    all_to_all x1, blocking collectives, shards(): out = lax.all_to_all(result, 'mode', 0, 0, tiled=True)  26.6 us
    all_to_all x1, waiting for transfers between devices, shards(): lax.all_to_all(jnp.concatenate([packed, extra], axis=1), 'mode', 0, 0, ti...  23.7 us
    ppermute x2, waiting for transfers between devices, swap(): lax.ppermute(onward, 'cell', shift_pairs(count, 1))  18 us
    ppermute x2, waiting for transfers between devices, swap(): lax.ppermute(back, 'cell', shift_pairs(count, -1))  7.93 us
    all_to_all x1, starting transfers between devices, shards(): lax.all_to_all(jnp.concatenate([packed, extra], axis=1), 'mode', 0, 0, ti...  7.79 us
    dot_general x2, matrix products, scatter(): lax.dot_general(field, scatter_matrix, (((2,), (1,)), ((), ())), preferre...  5.7 us
    ppermute x2, starting transfers between devices, swap(): lax.ppermute(back, 'cell', shift_pairs(count, -1))  5.53 us
    ppermute x2, starting transfers between devices, swap(): lax.ppermute(onward, 'cell', shift_pairs(count, 1))  5.3 us
  transfers between devices with their start and end apart: 5, of which 5 were waited for; matrix products, arithmetic and copies ran while one was open for 5% of the time, Pallas kernels for 0%

profile of v2, /device:TPU:257, one launch (start us, length us, event | category | flops | bytes accessed | tf_op | source)
XLA Modules:
  0.0 115.9 jit_solution(3337017207186291801)
XLA Ops:
  0.0 2.1 %convert_element_type.60 = bf16[96,2,2048]{2,1,0:T(2,128)(2,1)S(1)} convert(f32[96,2,2048]{2,1,0:T(2,128)} %param.7) | non-fusion elementwise | flops 393216 | bytes 2359296 | tf_op jit(solution)/shard_map/convert_element_type | solution.py:35
  2.1 0.5 reshape.113
  2.6 0.1 copy.48
  2.8 0.6 fusion.43
  3.4 0.7 copy.43
  4.0 0.7 copy.42
  4.9 0.8 copy.32
  5.7 0.5 reshape.103
  6.2 1.0 pad_maximum_fusion
  7.2 7.8 %all-to-all-start = ((bf16[16,104,256]{2,1,0:T(8,128)(2,1)}), bf16[16,104,256]{2,1,0:T(8,128)(2,1)S(1)}, u32[]{:S(2)}, u32[]{:S(2)}) async-start(bf16[16,104,256]{2,1,0:T(8,128)(2,1)} %pad_maximum_fusion), calls=%async_computation | async-start | bytes 1703936 | tf_op jit(solution)/shard_map/all_to_all | solution.py:47
  15.0 0.1 pad_dynamic-slice_fusion
  15.1 0.1 fusion.45
  15.1 0.1 slice_bitcast_fusion.5
  15.2 23.7 %all-to-all-done = bf16[16,104,256]{2,1,0:T(8,128)(2,1)S(1)} async-done(((bf16[16,104,256]{2,1,0:T(8,128)(2,1)}), bf16[16,104,256]{2,1,0:T(8,128)(2,1)S(1)}, u32[]{:S(2)}, u32[]{:S(2)}) %all-to-all-start) | async-done | bytes 852000 | tf_op jit(solution)/shard_map/all_to_all | solution.py:47
  39.0 0.1 reshape.107
  39.2 0.1 slice.145
  39.3 0.2 reshape.108
  39.5 0.6 copy.37
  40.1 0.1 slice_reduce_fusion.1
  40.2 0.1 mul.180
  40.3 0.1 mul.183
  40.4 0.1 max.35
  40.7 0.3 pad_maximum_fusion.1
  41.0 0.2 slice_bitcast_fusion.1
  41.2 3.5 %collective-permute-start.1 = (bf16[130,1536]{1,0:T(8,128)(2,1)S(1)}, bf16[130,1536]{1,0:T(8,128)(2,1)S(1)}, u32[]{:S(2)}, u32[]{:S(2)}) collective-permute-start(bf16[130,1536]{1,0:T(8,128)(2,1)S(1)} %get-tuple-element.22), channel_id=1, source_target_pairs={{1,0},{2,1},{3,2},{4,3},{5,4},{6,5},{7,6},{8,7},{9,8},{10,9},{11,1... | collective-permute-start | bytes 1198088 | tf_op jit(solution)/shard_map/ppermute | solution.py:19
  44.7 0.2 slice_multiply_fusion.5
  44.9 4.0 %fusion.19 = f32[2,130,1536]{2,1,0:T(8,128)S(1)} fusion(bf16[1536,1536]{1,0:T(8,128)(2,1)} %param.8, f32[2,132,1536]{2,1,0:T(8,128)S(1)} %get-tuple-element.24, f32[1,130,1536]{2,1,0:T(8,128)S(1)} %get-tuple-element.18, f32[1,130,1536]{2,1,0:T(8,128)S(1)} %get-tuple-element.17, bf16[2,132,1536]{2,1,0:T(8,128)(2,1)S(1)} %get-tuple-element.23, ...), kind=kOutput, calls=%fused_computation.9 | convolution fusion | flops 1230428160 | bytes 11944976 | tf_op jit(solution)/shard_map/dot_general | solution.py:65
  48.9 1.9 %collective-permute-start = (bf16[130,1536]{1,0:T(8,128)(2,1)S(1)}, bf16[130,1536]{1,0:T(8,128)(2,1)S(1)}, u32[]{:S(2)}, u32[]{:S(2)}) collective-permute-start(bf16[130,1536]{1,0:T(8,128)(2,1)S(1)} %get-tuple-element.21), channel_id=1, source_target_pairs={{0,1},{1,2},{2,3},{3,4},{4,5},{5,6},{6,7},{7,8},{8,9},{9,10},{10,1... | collective-permute-start | bytes 1198088 | tf_op jit(solution)/shard_map/ppermute | solution.py:18
  50.9 2.0 %collective-permute-done.1 = bf16[130,1536]{1,0:T(8,128)(2,1)S(1)} collective-permute-done((bf16[130,1536]{1,0:T(8,128)(2,1)S(1)}, bf16[130,1536]{1,0:T(8,128)(2,1)S(1)}, u32[]{:S(2)}, u32[]{:S(2)}) %collective-permute-start.1) | collective-permute-done | bytes 399392 | tf_op jit(solution)/shard_map/ppermute | solution.py:19
  52.9 0.1 multiply_bitcast_fusion
  53.0 11.3 %collective-permute-done = bf16[130,1536]{1,0:T(8,128)(2,1)S(1)} collective-permute-done((bf16[130,1536]{1,0:T(8,128)(2,1)S(1)}, bf16[130,1536]{1,0:T(8,128)(2,1)S(1)}, u32[]{:S(2)}, u32[]{:S(2)}) %collective-permute-start) | collective-permute-done | bytes 399392 | tf_op jit(solution)/shard_map/ppermute | solution.py:18
  64.3 0.1 multiply_bitcast_fusion.1
  64.4 0.3 fusion.42
  64.6 0.2 slice_multiply_fusion.7
  64.9 0.2 slice_bitcast_fusion.3
  65.1 2.1 %collective-permute-start.3 = (bf16[128,1536]{1,0:T(8,128)(2,1)S(1)}, bf16[128,1536]{1,0:T(8,128)(2,1)S(1)}, u32[]{:S(2)}, u32[]{:S(2)}) collective-permute-start(bf16[128,1536]{1,0:T(8,128)(2,1)S(1)} %get-tuple-element.20), channel_id=1, source_target_pairs={{1,0},{2,1},{3,2},{4,3},{5,4},{6,5},{7,6},{8,7},{9,8},{10,9},{11,1... | collective-permute-start | bytes 1179656 | tf_op jit(solution)/shard_map/ppermute | solution.py:19
  67.2 1.7 %fusion.31 = f32[2,128,1536]{2,1,0:T(8,128)S(1)} fusion(bf16[1536,1536]{1,0:T(8,128)(2,1)S(1)} %bitcast.76, f32[2,130,1536]{2,1,0:T(8,128)S(1)} %get-tuple-element.14, f32[1,128,1536]{2,1,0:T(8,128)S(1)} %get-tuple-element.16, f32[1,128,1536]{2,1,0:T(8,128)S(1)} %get-tuple-element.15, f32[1536]{0:T(1024)S(1)} %max.35, f32[1536]{0:T(1024)S(1)} %max.33, ...), kind=kOutput, calls=%fused_computation.13 | convolution fusion | flops 1211891712 | bytes 12616704 | tf_op jit(solution)/shard_map/dot_general | solution.py:65
  68.8 3.4 %collective-permute-start.2 = (bf16[128,1536]{1,0:T(8,128)(2,1)S(1)}, bf16[128,1536]{1,0:T(8,128)(2,1)S(1)}, u32[]{:S(2)}, u32[]{:S(2)}) collective-permute-start(bf16[128,1536]{1,0:T(8,128)(2,1)S(1)} %get-tuple-element.19), channel_id=1, source_target_pairs={{0,1},{1,2},{2,3},{3,4},{4,5},{5,6},{6,7},{7,8},{8,9},{9,10},{10,1... | collective-permute-start | bytes 1179656 | tf_op jit(solution)/shard_map/ppermute | solution.py:18
  72.2 5.9 %collective-permute-done.3 = bf16[128,1536]{1,0:T(8,128)(2,1)S(1)} collective-permute-done((bf16[128,1536]{1,0:T(8,128)(2,1)S(1)}, bf16[128,1536]{1,0:T(8,128)(2,1)S(1)}, u32[]{:S(2)}, u32[]{:S(2)}) %collective-permute-start.3) | collective-permute-done | bytes 393248 | tf_op jit(solution)/shard_map/ppermute | solution.py:19
  78.1 0.1 multiply_bitcast_fusion.2
  78.2 6.7 %collective-permute-done.2 = bf16[128,1536]{1,0:T(8,128)(2,1)S(1)} collective-permute-done((bf16[128,1536]{1,0:T(8,128)(2,1)S(1)}, bf16[128,1536]{1,0:T(8,128)(2,1)S(1)}, u32[]{:S(2)}, u32[]{:S(2)}) %collective-permute-start.2) | collective-permute-done | bytes 393248 | tf_op jit(solution)/shard_map/ppermute | solution.py:18
  84.9 0.1 multiply_bitcast_fusion.3
  85.0 0.3 fusion.36
  85.3 0.6 copy.38
  85.9 0.5 reshape.109
  86.4 26.6 %all_to_all.10 = bf16[16,96,256]{2,1,0:T(8,128)(2,1)S(1)} all-to-all(bf16[16,96,256]{2,1,0:T(8,128)(2,1)S(1)} %reshape.109), channel_id=1, replica_groups=mesh['mode'=16,'cell'=32] {'mode'}, dimensions={0} | all-to-all | bytes 1572864 | tf_op jit(solution)/shard_map/all_to_all | solution.py:93
  113.1 0.8 reshape.111
  113.8 2.0 %copy_bitcast_fusion = f32[96,2,2048]{2,1,0:T(2,128)} fusion(f32[16,96,2,128]{3,2,1,0:T(2,128)S(1)} %reshape.111), kind=kLoop, calls=%fused_computation.17 | loop fusion | bytes 3145728 | tf_op jit(solution)/shard_map/convert_element_type | solution.py:95
  (36 shorter events, 0.5 us)
Async XLA Ops:
  2.7 2.0 %copy-start.1 = (f32[96]{0:T(128)S(1)}, f32[96]{0:T(128)}, u32[]{:S(2)}) copy-start(f32[96]{0:T(128)} %param.10) | copy-start | bytes 1156
  2.7 2.0 %copy-start.2 = (f32[96]{0:T(128)S(1)}, f32[96]{0:T(128)}, u32[]{:S(2)}) copy-start(f32[96]{0:T(128)} %param.9) | copy-start | bytes 1156
  2.8 2.0 %copy-start.3 = (f32[96]{0:T(128)S(1)}, f32[96]{0:T(128)}, u32[]{:S(2)}) copy-start(f32[96]{0:T(128)} %param.11) | copy-start | bytes 1156
  2.8 2.0 %copy-start.4 = (f32[96]{0:T(128)S(1)}, f32[96]{0:T(128)}, u32[]{:S(2)}) copy-start(f32[96]{0:T(128)} %param.12) | copy-start | bytes 1156
  6.2 8.8 %copy-start = (s32[2,2048]{1,0:T(2,128)S(1)}, s32[2,2048]{1,0:T(2,128)}, u32[]{:S(2)}) copy-start(s32[2,2048]{1,0:T(2,128)} %param.13) | copy-start | bytes 49156
  7.2 31.8 %all-to-all-start = ((bf16[16,104,256]{2,1,0:T(8,128)(2,1)}), bf16[16,104,256]{2,1,0:T(8,128)(2,1)S(1)}, u32[]{:S(2)}, u32[]{:S(2)}) async-start(bf16[16,104,256]{2,1,0:T(8,128)(2,1)} %pad_maximum_fusion), calls=%async_computation | async-start | bytes 1703936 | tf_op jit(solution)/shard_map/all_to_all | solution.py:47
  41.2 11.7 %collective-permute-start.1 = (bf16[130,1536]{1,0:T(8,128)(2,1)S(1)}, bf16[130,1536]{1,0:T(8,128)(2,1)S(1)}, u32[]{:S(2)}, u32[]{:S(2)}) collective-permute-start(bf16[130,1536]{1,0:T(8,128)(2,1)S(1)} %get-tuple-element.22), channel_id=1, source_target_pairs={{1,0},{2,1},{3,2},{4,3},{5,4},{6,5},{7,6},{8,7},{9,8},{10,9},{11,1... | collective-permute-start | bytes 1198088 | tf_op jit(solution)/shard_map/ppermute | solution.py:19
  48.9 15.3 %collective-permute-start = (bf16[130,1536]{1,0:T(8,128)(2,1)S(1)}, bf16[130,1536]{1,0:T(8,128)(2,1)S(1)}, u32[]{:S(2)}, u32[]{:S(2)}) collective-permute-start(bf16[130,1536]{1,0:T(8,128)(2,1)S(1)} %get-tuple-element.21), channel_id=1, source_target_pairs={{0,1},{1,2},{2,3},{3,4},{4,5},{5,6},{6,7},{7,8},{8,9},{9,10},{10,1... | collective-permute-start | bytes 1198088 | tf_op jit(solution)/shard_map/ppermute | solution.py:18
  64.3 2.9 %slice-start = ((s8[4718592]{0:T(1024)(128)(4,1)}), s8[4194304]{0:T(1024)(128)(4,1)S(1)}, s32[]{:S(2)}) async-start(s8[4718592]{0:T(1024)(128)(4,1)} %bitcast.75), calls=%async_computation.2 | async-start | bytes 8388608
  64.3 2.8 %slice-start.1 = ((s8[4718592]{0:T(1024)(128)(4,1)}), s8[524288]{0:T(1024)(128)(4,1)S(1)}, s32[]{:S(2)}) async-start(s8[4718592]{0:T(1024)(128)(4,1)} %bitcast.75), calls=%async_computation.3 | async-start | bytes 1048576
  65.1 13.0 %collective-permute-start.3 = (bf16[128,1536]{1,0:T(8,128)(2,1)S(1)}, bf16[128,1536]{1,0:T(8,128)(2,1)S(1)}, u32[]{:S(2)}, u32[]{:S(2)}) collective-permute-start(bf16[128,1536]{1,0:T(8,128)(2,1)S(1)} %get-tuple-element.20), channel_id=1, source_target_pairs={{1,0},{2,1},{3,2},{4,3},{5,4},{6,5},{7,6},{8,7},{9,8},{10,9},{11,1... | collective-permute-start | bytes 1179656 | tf_op jit(solution)/shard_map/ppermute | solution.py:19
  68.8 16.1 %collective-permute-start.2 = (bf16[128,1536]{1,0:T(8,128)(2,1)S(1)}, bf16[128,1536]{1,0:T(8,128)(2,1)S(1)}, u32[]{:S(2)}, u32[]{:S(2)}) collective-permute-start(bf16[128,1536]{1,0:T(8,128)(2,1)S(1)} %get-tuple-element.19), channel_id=1, source_target_pairs={{0,1},{1,2},{2,3},{3,4},{4,5},{5,6},{6,7},{7,8},{8,9},{9,10},{10,1... | collective-permute-start | bytes 1179656 | tf_op jit(solution)/shard_map/ppermute | solution.py:18

commit v3 on v0

v3 whole, which is shorter than its diff:
```python
import jax
import jax.numpy as jnp
from jax import lax
from jax.experimental import pallas as pl
from jax.experimental.pallas import tpu as pltpu
from jax.sharding import PartitionSpec as P

F32 = jnp.float32
BF16 = jnp.bfloat16
SIDE = 8
TILE = 256
MIB = 1024 * 1024


def shift_pairs(count, step):
    return [(i, i + step) for i in range(count) if 0 <= i + step < count]


def swap(onward, back):
    count = lax.axis_size("cell")
    return (
        lax.ppermute(onward, "cell", shift_pairs(count, 1)),
        lax.ppermute(back, "cell", shift_pairs(count, -1)),
    )


IN_VMEM = pl.BlockSpec(memory_space=pltpu.VMEM)
IN_HBM = pl.BlockSpec(memory_space=pltpu.HBM)


def params(limit):
    return pltpu.CompilerParams(vmem_limit_bytes=limit * MIB)


def iota(shape, axis):
    return lax.broadcasted_iota(jnp.int32, shape, axis)


def pack_body(speed_x_in, speed_y_in, relaxation_in, emission_in, initial_in, packed, *scratch):
    arrived = scratch[-1]
    sources = (speed_x_in, speed_y_in, relaxation_in, emission_in, initial_in)
    copies = [
        pltpu.make_async_copy(source, place, arrived.at[k])
        for k, (source, place) in enumerate(zip(sources, scratch[:-1]))
    ]
    for copy in copies:
        copy.start()
    for copy in copies:
        copy.wait()
    speed_x, speed_y, relaxation, emission, initial = scratch[:-1]
    groups, height, cells = packed.shape
    modes, span = height - SIDE, cells // 2
    sx, sy = speed_x[...], speed_y[...]
    inverse = 1.0 / (relaxation[...] + jnp.abs(sx) + jnp.abs(sy))
    vectors = jnp.concatenate([sx * inverse, sy * inverse, inverse, emission[...] * inverse], axis=0)
    high = vectors.astype(BF16).astype(F32)
    vectors = jnp.concatenate([high, vectors - high], axis=0)
    vectors = jnp.concatenate([vectors, jnp.zeros((SIDE, span - modes), F32)], axis=1)
    row, lane = iota((SIDE, cells), 0), iota((SIDE, cells), 1)
    pair, odd = row // 2, row % 2
    column = ((pair == 1) | (pair == 2)).astype(jnp.int32)
    after = (pair == 0) | (pair == 2)
    pick = lane == column * span + jnp.where(after, odd, span - 2 + odd)
    pick = jnp.where(pick, 1.0, 0.0).astype(BF16)
    is_after = ((iota((SIDE, span), 0) // 2) % 2) == 0
    ends = []
    for group in range(groups):
        at = pl.ds(group * span, span)
        block = jnp.concatenate([initial[:, c, at] for c in range(2)], axis=1).astype(BF16)
        packed[group, :modes, :] = block
        block = jnp.concatenate([block, jnp.zeros((span - modes, cells), BF16)], axis=0)
        ends.append(
            lax.dot_general(pick, block, (((1,), (1,)), ((), ())), preferred_element_type=F32)
        )
    none = jnp.zeros((SIDE, span), F32)
    for group in range(groups):
        after = ends[group + 1] if group + 1 < groups else none
        before = ends[group - 1] if group else none
        edge = jnp.where(is_after, after, before)
        packed[group, modes:, :] = jnp.concatenate([edge, vectors], axis=1).astype(BF16)


def pack(initial, vectors, groups):
    modes, cols, length = initial.shape
    shape = (groups, modes + SIDE, cols * length // groups)
    return pl.pallas_call(
        pack_body,
        in_specs=[IN_HBM] * 5,
        out_specs=IN_VMEM,
        scratch_shapes=[pltpu.VMEM((1, modes), F32)] * 4
        + [pltpu.VMEM(initial.shape, F32), pltpu.SemaphoreType.DMA((5,))],
        out_shape=jax.ShapeDtypeStruct(shape, BF16),
        compiler_params=params(32),
        cost_estimate=pl.CostEstimate(flops=10**7, bytes_accessed=3 * MIB, transcendentals=0),
        name="pack",
    )(*[v[None] for v in vectors], initial)


def unpack_body(received, own_0, own_1, coef):
    groups, height, cells = received.shape
    modes, span = height - SIDE, cells // 2
    unit = jnp.where(iota((span, span), 0) == iota((span, span), 1), 1.0, 0.0).astype(BF16)
    together = 4
    wide = together * modes
    for first in range(0, groups, together):
        lanes = pl.ds(first // together * wide, wide)
        members = range(first, first + together)
        edge = jnp.concatenate([received[j, modes:, :modes] for j in members], axis=1).astype(F32)
        vector = jnp.concatenate(
            [received[j, modes:, span : span + modes] for j in members], axis=1
        ).astype(F32)
        coef[:, lanes] = vector + pltpu.roll(vector, 4, 0)
        for c, out in ((0, own_0), (1, own_1)):
            block = jnp.concatenate(
                [received[j, :modes, c * span : (c + 1) * span] for j in members], axis=0
            )
            turned = lax.dot_general(
                unit, block, (((1,), (1,)), ((), ())), preferred_element_type=F32
            )
            ends = edge if c == 0 else pltpu.roll(edge, 4, 0)
            out[:, lanes] = jnp.concatenate([turned, ends], axis=0).astype(BF16)


def unpack(received):
    groups, height, cells = received.shape
    total, rows = groups * (height - SIDE), cells // 2 + SIDE
    return pl.pallas_call(
        unpack_body,
        out_shape=[jax.ShapeDtypeStruct((rows, total), BF16)] * 2
        + [jax.ShapeDtypeStruct((SIDE, total), F32)],
        compiler_params=params(32),
        cost_estimate=pl.CostEstimate(flops=10**7, bytes_accessed=3 * MIB, transcendentals=0),
        name="unpack",
    )(received)


def scatter(matrix, values):
    return lax.dot_general(
        values, matrix, (((1,), (0,)), ((), ())), preferred_element_type=F32
    )


def local_terms(scattered, mine, other, x_rate, coef, heat):
    rows, kept = mine.shape[0], scattered.shape[0]
    y_rate, inverse, emit = (coef[k : k + 1, :] for k in (1, 2, 3))
    return (
        scattered * inverse
        + heat * emit
        + jnp.maximum(y_rate, 0.0) * pltpu.roll(mine, 1, 0)[:kept]
        + jnp.maximum(-y_rate, 0.0) * pltpu.roll(mine, rows - 1, 0)[:kept]
        + x_rate * other[:kept]
    )


def first_body(own_0, own_1, matrix, coef, heat, part_0, part_1, sent_0, sent_1, both):
    rows, total = own_0.shape
    both[:rows, :] = own_0[...].astype(F32).astype(BF16)
    both[rows:, :] = own_1[...].astype(F32).astype(BF16)
    for first in range(0, total, TILE):
        at = pl.ds(first, TILE)
        x_rate = coef[0:1, at]
        wide_0, wide_1 = own_0[:, at].astype(F32), own_1[:, at].astype(F32)
        scattered = scatter(matrix[:, at], both[...])
        value = local_terms(
            scattered[:rows], wide_0, wide_1, jnp.maximum(-x_rate, 0.0), coef[:, at], heat[0]
        )
        part_0[:, at] = value
        sent_0[:, at] = value.astype(BF16)
        value = local_terms(
            scattered[rows:], wide_1, wide_0, jnp.maximum(x_rate, 0.0), coef[:, at], heat[1]
        )
        part_1[:, at] = value
        sent_1[:, at] = value.astype(BF16)


def first_step(own_0, own_1, matrix, coef, heat):
    rows, total = own_0.shape
    return pl.pallas_call(
        first_body,
        in_specs=[IN_VMEM] * 5,
        out_specs=[IN_VMEM] * 4,
        out_shape=[jax.ShapeDtypeStruct((rows, total), F32)] * 2
        + [jax.ShapeDtypeStruct((rows, total), BF16)] * 2,
        scratch_shapes=[pltpu.VMEM((2 * rows, total), BF16)],
        compiler_params=params(24),
        cost_estimate=pl.CostEstimate(
            flops=4 * rows * total * total, bytes_accessed=8 * MIB, transcendentals=0
        ),
        name="first_step",
    )(own_0, own_1, matrix, coef, heat)


def second_body(part_0, part_1, left, right, matrix, coef, heat, base_0, base_1, field, narrow):
    span, total = base_0.shape
    x_rate = coef[0:1, :]
    field[0] = part_0[...] + jnp.maximum(x_rate, 0.0) * left[...].astype(F32)
    field[1] = part_1[...] + jnp.maximum(-x_rate, 0.0) * right[...].astype(F32)
    for c in range(2):
        narrow[c * span : (c + 1) * span, :] = field[c, :span, :].astype(BF16)
    for first in range(0, total, TILE):
        at = pl.ds(first, TILE)
        x_rate = coef[0:1, at]
        scattered = scatter(matrix[:, at], narrow[...])
        mine_0, mine_1 = field[0, :, at], field[1, :, at]
        base_0[:, at] = local_terms(
            scattered[:span], mine_0, mine_1, jnp.maximum(-x_rate, 0.0), coef[:, at], heat[0, :span]
        )
        base_1[:, at] = local_terms(
            scattered[span:], mine_1, mine_0, jnp.maximum(x_rate, 0.0), coef[:, at], heat[1, :span]
        )


def second_step(part_0, part_1, left, right, matrix, coef, heat):
    rows, total = part_0.shape
    span = rows - SIDE
    return pl.pallas_call(
        second_body,
        in_specs=[IN_VMEM] * 7,
        out_specs=[IN_VMEM] * 2,
        out_shape=[jax.ShapeDtypeStruct((span, total), F32)] * 2,
        scratch_shapes=[pltpu.VMEM((2, rows, total), F32), pltpu.VMEM((2 * span, total), BF16)],
        compiler_params=params(24),
        cost_estimate=pl.CostEstimate(
            flops=4 * rows * total * total, bytes_accessed=8 * MIB, transcendentals=0
        ),
        name="second_step",
    )(part_0, part_1, left, right, matrix, coef, heat)


def finish_body(base_0, base_1, left, right, coef, result):
    groups, modes, cells = result.shape
    span = cells // 2
    unit = jnp.where(iota((span, span), 0) == iota((span, span), 1), 1.0, 0.0).astype(BF16)
    together = 4
    wide = together * modes
    for first in range(0, groups, together):
        lanes = pl.ds(first // together * wide, wide)
        x_rate = coef[0:1, lanes]
        for c, base, outer, rate in (
            (0, base_0, left, jnp.maximum(x_rate, 0.0)),
            (1, base_1, right, jnp.maximum(-x_rate, 0.0)),
        ):
            value = base[:, lanes] + rate * outer[:span, lanes].astype(F32)
            turned = lax.dot_general(
                value.astype(BF16), unit, (((0,), (0,)), ((), ())), preferred_element_type=F32
            ).astype(BF16)
            for k in range(together):
                result[first + k, :, c * span : (c + 1) * span] = turned[k * modes : (k + 1) * modes]


def finish(base_0, base_1, left, right, coef, groups):
    span, total = base_0.shape
    return pl.pallas_call(
        finish_body,
        out_shape=jax.ShapeDtypeStruct((groups, total // groups, 2 * span), BF16),
        compiler_params=params(32),
        cost_estimate=pl.CostEstimate(flops=10**7, bytes_accessed=3 * MIB, transcendentals=0),
        name="finish",
    )(base_0, base_1, left, right, coef)


def shards(initial, scatter_matrix, speed_x, speed_y, relaxation, emission, heater):
    modes, cols, length = initial.shape
    groups = lax.axis_size("mode")
    span = length // groups

    turned = lax.optimization_barrier(scatter_matrix.T)
    packed = pack(initial, (speed_x, speed_y, relaxation, emission), groups)
    received = lax.all_to_all(packed, "mode", 0, 0, tiled=True)
    own_0, own_1, coef = unpack(received)

    heat = jnp.pad(heater.astype(F32), ((0, 0), (2, 2)))
    heat = lax.dynamic_slice_in_dim(heat, lax.axis_index("mode") * span, span + 4, axis=1)
    none = jnp.zeros((cols, 4), F32)
    heat = jnp.concatenate([heat[:, 2:], none, heat[:, :2]], axis=1)[:, :, None]

    left, right = swap(own_1, own_0)
    part_0, part_1, sent_0, sent_1 = first_step(own_0, own_1, turned, coef, heat)
    left_2, right_2 = swap(sent_1, sent_0)
    base_0, base_1 = second_step(part_0, part_1, left, right, turned, coef, heat)
    result = finish(base_0, base_1, left_2, right_2, coef, groups)

    out = lax.all_to_all(result, "mode", 0, 0, tiled=True)
    out = out.reshape(groups, modes, cols, span).transpose(1, 2, 0, 3)
    return out.reshape(modes, cols, length).astype(F32)


def solution(mesh):
    return jax.shard_map(
        shards,
        mesh=mesh,
        in_specs=(
            P("mode", "cell", None),
            P(),
            P("mode"),
            P("mode"),
            P("mode"),
            P("mode"),
            P("cell", None),
        ),
        out_specs=P("mode", "cell", None),
        check_vma=False,
    )
```

time: 193 us -> 100 us (0.52)
  the two profiles are of different devices: /device:TPU:1 before, /device:TPU:199 now
where the time goes in v3:
time: 100 us; the launch traced here: 99.7 us
  waiting for transfers between devices  27.5 us (28%)
  blocking collectives  27.1 us (27%)
  starting transfers between devices  21.7 us (22%)
  local copies, waits for them, and re-layouts  16.2 us (16%)
  Pallas kernels  6.99 us (7%)
    all_to_all x1, blocking collectives, shards(): out = lax.all_to_all(result, 'mode', 0, 0, tiled=True)  27.1 us
    all_to_all x1, waiting for transfers between devices, shards(): received = lax.all_to_all(packed, 'mode', 0, 0, tiled=True)  16.8 us
    unnamed x17, local copies, waits for them, and re-layouts  13 us
    ppermute x2, starting transfers between devices, swap(): lax.ppermute(onward, 'cell', shift_pairs(count, 1))  8.07 us
    all_to_all x1, starting transfers between devices, shards(): received = lax.all_to_all(packed, 'mode', 0, 0, tiled=True)  7.8 us
    ppermute x2, waiting for transfers between devices, swap(): lax.ppermute(onward, 'cell', shift_pairs(count, 1))  5.88 us
    ppermute x2, starting transfers between devices, swap(): lax.ppermute(back, 'cell', shift_pairs(count, -1))  5.82 us
    ppermute x2, waiting for transfers between devices, swap(): lax.ppermute(back, 'cell', shift_pairs(count, -1))  4.78 us
  transfers between devices with their start and end apart: 5, of which 3 were waited for; matrix products, arithmetic and copies ran while one was open for 7% of the time, Pallas kernels for 4%

profile of v3, /device:TPU:199, one launch (start us, length us, event | category | flops | bytes accessed | tf_op | source)
XLA Modules:
  0.0 99.7 jit_solution(15292932720740070514)
XLA Ops:
  0.0 0.0 copy-start.2
  0.0 1.4 %copy-done.2 = f32[96,2,2048]{2,1,0:T(2,128)S(1)} copy-done((f32[96,2,2048]{2,1,0:T(2,128)S(1)}, f32[96,2,2048]{2,1,0:T(2,128)}, u32[]{:S(2)}) %copy-start.2) | copy-done | bytes 1572888
  1.4 0.0 copy-start.3
  1.4 0.7 copy-done.3
  2.1 0.0 copy-start.4
  2.1 0.7 copy-done.4
  2.7 0.0 copy-start.5
  2.7 0.7 copy-done.5
  3.4 0.0 copy-start.6
  3.4 0.7 copy-done.6
  4.0 0.0 copy-start.7
  4.0 2.5 %pack.1 = bf16[16,104,256]{2,1,0:T(8,128)(2,1)} custom-call(f32[1,96]{1,0:T(1,128)S(1)} %bitcast.15, f32[1,96]{1,0:T(1,128)S(1)} %bitcast.16, f32[1,96]{1,0:T(1,128)S(1)} %bitcast.17, f32[1,96]{1,0:T(1,128)S(1)} %bitcast.18, f32[96,2,2048]{2,1,0:T(2,128)S(1)} %copy-done.2), custom_call_target="tpu_custom_call" | custom-call | flops 10000000 | bytes 3145728 | tf_op jit(solution)/shard_map/pack/pallas_call | solution.py:86
  6.6 7.8 %all-to-all-start = ((bf16[16,104,256]{2,1,0:T(8,128)(2,1)}), bf16[16,104,256]{2,1,0:T(8,128)(2,1)S(1)}, u32[]{:S(2)}, u32[]{:S(2)}) async-start(bf16[16,104,256]{2,1,0:T(8,128)(2,1)} %pack.1), calls=%async_computation | async-start | bytes 1703936 | tf_op jit(solution)/shard_map/all_to_all | solution.py:269
  14.4 0.0 copy-done.7
  14.4 0.1 pad.6.clone
  14.5 0.1 pad_dynamic-slice_fusion.1
  14.5 0.1 pad_dynamic-slice_fusion
  14.6 0.1 maximum_bitcast_fusion
  14.7 0.1 copy.11.heat
  14.8 6.6 %copy.10 = bf16[1536,1536]{0,1:T(8,128)(2,1)} copy(bf16[1536,1536]{1,0:T(8,128)(2,1)} %param.8) | data formatting | bytes 9437184 | tf_op args[1]
  21.5 16.8 %all-to-all-done.received = bf16[16,104,256]{2,1,0:T(8,128)(2,1)S(1)} async-done(((bf16[16,104,256]{2,1,0:T(8,128)(2,1)}), bf16[16,104,256]{2,1,0:T(8,128)(2,1)S(1)}, u32[]{:S(2)}, u32[]{:S(2)}) %all-to-all-start) | async-done | bytes 852000 | tf_op jit(solution)/shard_map/all_to_all | solution.py:269
  38.3 0.5 unpack.1
  38.8 2.5 %collective-permute-start.1 = (bf16[136,1536]{1,0:T(8,128)(2,1)S(1)}, bf16[136,1536]{1,0:T(8,128)(2,1)S(1)}, u32[]{:S(2)}, u32[]{:S(2)}) collective-permute-start(bf16[136,1536]{1,0:T(8,128)(2,1)S(1)} %get-tuple-element.14.own_0), channel_id=1, source_target_pairs={{1,0},{2,1},{3,2},{4,3},{5,4},{6,5},{7,6},{8,7},{9,8},{10,9},{11,1... | collective-permute-start | bytes 1253384 | tf_op jit(solution)/shard_map/ppermute | solution.py:23
  41.3 6.1 %collective-permute-start = (bf16[136,1536]{1,0:T(8,128)(2,1)S(1)}, bf16[136,1536]{1,0:T(8,128)(2,1)S(1)}, u32[]{:S(2)}, u32[]{:S(2)}) collective-permute-start(bf16[136,1536]{1,0:T(8,128)(2,1)S(1)} %get-tuple-element.15.own_1), channel_id=1, source_target_pairs={{0,1},{1,2},{2,3},{3,4},{4,5},{5,6},{6,7},{7,8},{8,9},{9,10},{10,1... | collective-permute-start | bytes 1253384 | tf_op jit(solution)/shard_map/ppermute | solution.py:22
  47.4 0.0 copy-start
  47.4 2.3 %copy-done = bf16[1536,1536]{0,1:T(8,128)(2,1)S(1)} copy-done((bf16[1536,1536]{0,1:T(8,128)(2,1)S(1)}, bf16[1536,1536]{0,1:T(8,128)(2,1)}, u32[]{:S(2)}) %copy-start) | copy-done | bytes 4718616
  49.7 0.0 copy-start.1
  49.8 1.9 %first_step.1 = (f32[136,1536]{1,0:T(8,128)S(1)}, f32[136,1536]{1,0:T(8,128)S(1)}, bf16[136,1536]{1,0:T(8,128)(2,1)S(1)}, bf16[136,1536]{1,0:T(8,128)(2,1)S(1)}) custom-call(bf16[136,1536]{1,0:T(8,128)(2,1)S(1)} %get-tuple-element.14.own_0, bf16[136,1536]{1,0:T(8,128)(2,1)S(1)} %get-tuple-element.15.own_1, bf16[1536,1536]{1,0:T(8,128)(2,1)S(1)} %bitcast.13, ...), custom_call_target="tpu_custom_call" | custom-call | flops 1283457024 | bytes 8388608 | tf_op jit(solution)/shard_map/first_step/pallas_call | solution.py:178
  51.6 1.9 %collective-permute-start.2 = (bf16[136,1536]{1,0:T(8,128)(2,1)S(1)}, bf16[136,1536]{1,0:T(8,128)(2,1)S(1)}, u32[]{:S(2)}, u32[]{:S(2)}) collective-permute-start(bf16[136,1536]{1,0:T(8,128)(2,1)S(1)} %get-tuple-element.21), channel_id=1, source_target_pairs={{0,1},{1,2},{2,3},{3,4},{4,5},{5,6},{6,7},{7,8},{8,9},{9,10},{10,1... | collective-permute-start | bytes 1253384 | tf_op jit(solution)/shard_map/ppermute | solution.py:22
  53.6 3.4 %collective-permute-start.3 = (bf16[136,1536]{1,0:T(8,128)(2,1)S(1)}, bf16[136,1536]{1,0:T(8,128)(2,1)S(1)}, u32[]{:S(2)}, u32[]{:S(2)}) collective-permute-start(bf16[136,1536]{1,0:T(8,128)(2,1)S(1)} %get-tuple-element.22), channel_id=1, source_target_pairs={{1,0},{2,1},{3,2},{4,3},{5,4},{6,5},{7,6},{8,7},{9,8},{10,9},{11,1... | collective-permute-start | bytes 1253384 | tf_op jit(solution)/shard_map/ppermute | solution.py:23
  56.9 0.0 collective-permute-done.1.right
  56.9 0.0 collective-permute-done.left
  56.9 0.0 copy-done.1
  57.0 1.7 %second_step.1 = (f32[128,1536]{1,0:T(8,128)S(1)}, f32[128,1536]{1,0:T(8,128)S(1)}) custom-call(f32[136,1536]{1,0:T(8,128)S(1)} %get-tuple-element.17.part_0, f32[136,1536]{1,0:T(8,128)S(1)} %get-tuple-element.18.part_1, bf16[136,1536]{1,0:T(8,128)(2,1)S(1)} %collective-permute-done.left, bf16[136,1536]{1,0:T(8,128)(2,1)S(1)} %collective-permute-done.1.right, ...), custom_call_target="tpu_custom_call" | custom-call | flops 1283457024 | bytes 8388608 | tf_op jit(solution)/shard_map/second_step/pallas_call | solution.py:216
  58.7 5.9 %collective-permute-done.2.left = bf16[136,1536]{1,0:T(8,128)(2,1)S(1)} collective-permute-done((bf16[136,1536]{1,0:T(8,128)(2,1)S(1)}, bf16[136,1536]{1,0:T(8,128)(2,1)S(1)}, u32[]{:S(2)}, u32[]{:S(2)}) %collective-permute-start.2) | collective-permute-done | bytes 417824 | tf_op jit(solution)/shard_map/ppermute | solution.py:22
  64.6 4.8 %collective-permute-done.3.right = bf16[136,1536]{1,0:T(8,128)(2,1)S(1)} collective-permute-done((bf16[136,1536]{1,0:T(8,128)(2,1)S(1)}, bf16[136,1536]{1,0:T(8,128)(2,1)S(1)}, u32[]{:S(2)}, u32[]{:S(2)}) %collective-permute-start.3) | collective-permute-done | bytes 417824 | tf_op jit(solution)/shard_map/ppermute | solution.py:23
  69.3 0.4 finish.1
  69.8 27.1 %all_to_all.10 = bf16[16,96,256]{2,1,0:T(8,128)(2,1)S(1)} all-to-all(bf16[16,96,256]{2,1,0:T(8,128)(2,1)S(1)} %finish.1), channel_id=1, replica_groups=mesh['mode'=16,'cell'=32] {'mode'}, dimensions={0} | all-to-all | bytes 1572864 | tf_op jit(solution)/shard_map/all_to_all | solution.py:283
  96.9 0.8 reshape.7
  97.6 2.0 %copy_bitcast_fusion = f32[96,2,2048]{2,1,0:T(2,128)} fusion(f32[16,96,2,128]{3,2,1,0:T(2,128)S(1)} %reshape.7), kind=kLoop, calls=%fused_computation | loop fusion | bytes 3145728 | tf_op jit(solution)/shard_map/convert_element_type | solution.py:285
  (2 shorter events, 0.0 us)
Async XLA Ops:
  0.0 1.4 %copy-start.2 = (f32[96,2,2048]{2,1,0:T(2,128)S(1)}, f32[96,2,2048]{2,1,0:T(2,128)}, u32[]{:S(2)}) copy-start(f32[96,2,2048]{2,1,0:T(2,128)} %initial_in.1) | copy-start | bytes 4718596
  1.4 0.7 copy-start.3
  2.1 0.7 copy-start.4
  2.7 0.7 copy-start.5
  3.4 0.7 copy-start.6
  4.0 10.3 %copy-start.7 = (s32[2,2048]{1,0:T(2,128)S(1)}, s32[2,2048]{1,0:T(2,128)}, u32[]{:S(2)}) copy-start(s32[2,2048]{1,0:T(2,128)} %param.13) | copy-start | bytes 49156
  6.6 31.8 %all-to-all-start = ((bf16[16,104,256]{2,1,0:T(8,128)(2,1)}), bf16[16,104,256]{2,1,0:T(8,128)(2,1)S(1)}, u32[]{:S(2)}, u32[]{:S(2)}) async-start(bf16[16,104,256]{2,1,0:T(8,128)(2,1)} %pack.1), calls=%async_computation | async-start | bytes 1703936 | tf_op jit(solution)/shard_map/all_to_all | solution.py:269
  38.8 18.1 %collective-permute-start.1 = (bf16[136,1536]{1,0:T(8,128)(2,1)S(1)}, bf16[136,1536]{1,0:T(8,128)(2,1)S(1)}, u32[]{:S(2)}, u32[]{:S(2)}) collective-permute-start(bf16[136,1536]{1,0:T(8,128)(2,1)S(1)} %get-tuple-element.14.own_0), channel_id=1, source_target_pairs={{1,0},{2,1},{3,2},{4,3},{5,4},{6,5},{7,6},{8,7},{9,8},{10,9},{11,1... | collective-permute-start | bytes 1253384 | tf_op jit(solution)/shard_map/ppermute | solution.py:23
  41.3 15.7 %collective-permute-start = (bf16[136,1536]{1,0:T(8,128)(2,1)S(1)}, bf16[136,1536]{1,0:T(8,128)(2,1)S(1)}, u32[]{:S(2)}, u32[]{:S(2)}) collective-permute-start(bf16[136,1536]{1,0:T(8,128)(2,1)S(1)} %get-tuple-element.15.own_1), channel_id=1, source_target_pairs={{0,1},{1,2},{2,3},{3,4},{4,5},{5,6},{6,7},{7,8},{8,9},{9,10},{10,1... | collective-permute-start | bytes 1253384 | tf_op jit(solution)/shard_map/ppermute | solution.py:22
  47.4 2.3 %copy-start = (bf16[1536,1536]{0,1:T(8,128)(2,1)S(1)}, bf16[1536,1536]{0,1:T(8,128)(2,1)}, u32[]{:S(2)}) copy-start(bf16[1536,1536]{0,1:T(8,128)(2,1)} %copy.10) | copy-start | bytes 14155780
  49.7 7.2 %copy-start.1 = (bf16[1536,1536]{0,1:T(8,128)(2,1)S(1)}, bf16[1536,1536]{0,1:T(8,128)(2,1)}, u32[]{:S(2)}) copy-start(bf16[1536,1536]{0,1:T(8,128)(2,1)} %copy.10) | copy-start | bytes 14155780
  51.6 12.9 %collective-permute-start.2 = (bf16[136,1536]{1,0:T(8,128)(2,1)S(1)}, bf16[136,1536]{1,0:T(8,128)(2,1)S(1)}, u32[]{:S(2)}, u32[]{:S(2)}) collective-permute-start(bf16[136,1536]{1,0:T(8,128)(2,1)S(1)} %get-tuple-element.21), channel_id=1, source_target_pairs={{0,1},{1,2},{2,3},{3,4},{4,5},{5,6},{6,7},{7,8},{8,9},{9,10},{10,1... | collective-permute-start | bytes 1253384 | tf_op jit(solution)/shard_map/ppermute | solution.py:22
  53.6 15.8 %collective-permute-start.3 = (bf16[136,1536]{1,0:T(8,128)(2,1)S(1)}, bf16[136,1536]{1,0:T(8,128)(2,1)S(1)}, u32[]{:S(2)}, u32[]{:S(2)}) collective-permute-start(bf16[136,1536]{1,0:T(8,128)(2,1)S(1)} %get-tuple-element.22), channel_id=1, source_target_pairs={{1,0},{2,1},{3,2},{4,3},{5,4},{6,5},{7,6},{8,7},{9,8},{10,9},{11,1... | collective-permute-start | bytes 1253384 | tf_op jit(solution)/shard_map/ppermute | solution.py:23

commit v4 on v3

v4 whole, which is shorter than its diff:
```python
import jax
import jax.numpy as jnp
from jax import lax
from jax.experimental import pallas as pl
from jax.experimental.pallas import tpu as pltpu
from jax.sharding import PartitionSpec as P

F32 = jnp.float32
BF16 = jnp.bfloat16
SIDE = 8
TILE = 256
MIB = 1024 * 1024
PIECES = 4
PACK_LIMIT = 62


def swap(to_first, to_second):
    count = lax.axis_size("cell")
    first = [(i, i ^ 1) for i in range(count)]
    second = [(i, i + 1 if i % 2 else i - 1) for i in range(count)]
    inside = lambda pairs: [(i, j) for i, j in pairs if 0 <= j < count]
    return (
        lax.ppermute(to_first, "cell", inside(first)),
        lax.ppermute(to_second, "cell", inside(second)),
    )


IN_VMEM = pl.BlockSpec(memory_space=pltpu.VMEM)
IN_HBM = pl.BlockSpec(memory_space=pltpu.HBM)


def params(limit):
    return pltpu.CompilerParams(vmem_limit_bytes=limit * MIB)


def one_hot(mask):
    return jnp.where(mask, 1.0, 0.0).astype(BF16)


def iota(shape, axis):
    return lax.broadcasted_iota(jnp.int32, shape, axis)


def pack_body(
    speed_x_in, speed_y_in, relaxation_in, emission_in, initial_in, packed,
    speed_x, speed_y, relaxation, emission, initial, arrived,
):
    groups, height, cells = packed.shape
    modes, span = height - SIDE, cells // 2
    per = groups // PIECES
    pairs = ((speed_x_in, speed_x), (speed_y_in, speed_y), (relaxation_in, relaxation), (emission_in, emission))
    small = [pltpu.make_async_copy(*pair, arrived.at[k]) for k, pair in enumerate(pairs)]
    large = []
    for k in range(PIECES):
        at = pl.ds(k * per * span, per * span)
        large.append(
            pltpu.make_async_copy(initial_in.at[:, :, at], initial.at[:, :, at], arrived.at[4 + k])
        )
    for copy in large[:1] + small + large[1:]:
        copy.start()
    wide = 2 * modes
    row, lane = iota((wide, wide), 0), iota((wide, wide), 1)
    apart = one_hot(lane == jnp.where(row < modes, 2 * row, 2 * (row - modes) + 1))
    row, lane = iota((per * span, groups * SIDE), 0), iota((per * span, groups * SIDE), 1)
    after = (lane // 2) % 2 == 0
    target = lane // SIDE * span + lane % 2 + jnp.where(after, span, -2) - row
    ends = jnp.zeros((wide, groups * SIDE), F32)
    for k in range(PIECES):
        large[k].wait()
        first = k * per * span
        both = [
            initial[:, :, pl.ds(first + g * span, span)].reshape(wide, span).astype(BF16)
            for g in range(per)
        ]
        both = jnp.concatenate(both, axis=1)
        ends += jnp.dot(both, one_hot(target == first), preferred_element_type=F32)
        both = jnp.dot(apart, both, preferred_element_type=F32).astype(BF16)
        for g in range(per):
            at = slice(g * span, (g + 1) * span)
            packed[k * per + g, :modes, :] = jnp.concatenate([both[:modes, at], both[modes:, at]], axis=1)
    ends = jnp.dot(apart, ends.astype(BF16), preferred_element_type=F32)
    ends = jnp.concatenate(
        [ends[:modes], jnp.zeros((span - modes, groups * SIDE), F32),
         ends[modes:], jnp.zeros((span - modes, groups * SIDE), F32)], axis=0
    ).T
    middle = (iota((groups * SIDE, span), 0) % SIDE) // 2
    ends = jnp.where((middle == 1) | (middle == 2), ends[:, span:], ends[:, :span])
    for copy in small:
        copy.wait()
    sx, sy = speed_x[...], speed_y[...]
    inverse = 1.0 / (relaxation[...] + jnp.abs(sx) + jnp.abs(sy))
    vectors = jnp.concatenate([sx * inverse, sy * inverse, inverse, emission[...] * inverse], axis=0)
    high = vectors.astype(BF16).astype(F32)
    vectors = jnp.concatenate([high, vectors - high], axis=0)
    vectors = jnp.concatenate([vectors, jnp.zeros((SIDE, span - modes), F32)], axis=1)
    for group in range(groups):
        edge = ends[group * SIDE : (group + 1) * SIDE]
        packed[group, modes:, :] = jnp.concatenate([edge, vectors], axis=1).astype(BF16)


def pack(initial, vectors, groups):
    modes, cols, length = initial.shape
    shape = (groups, modes + SIDE, cols * length // groups)
    return pl.pallas_call(
        pack_body,
        in_specs=[IN_HBM] * 5,
        out_specs=IN_VMEM,
        scratch_shapes=[pltpu.VMEM((1, modes), F32)] * 4
        + [pltpu.VMEM(initial.shape, F32), pltpu.SemaphoreType.DMA((4 + PIECES,))],
        out_shape=jax.ShapeDtypeStruct(shape, BF16),
        compiler_params=params(PACK_LIMIT),
        cost_estimate=pl.CostEstimate(flops=10**7, bytes_accessed=3 * MIB, transcendentals=0),
        name="pack",
    )(*[v[None] for v in vectors], initial)


def unpack_body(received, heater, own_0, own_1, coef, heat):
    groups, height, cells = received.shape
    modes, span = height - SIDE, cells // 2
    unit = one_hot(iota((span, span), 0) == iota((span, span), 1))
    me = lax.axis_index("mode")
    even = lax.axis_index("cell") % 2 == 0
    parts = []
    for k in (-1, 0, 1):
        there = me + k
        inside = ((there >= 0) & (there < groups)).astype(jnp.int32)
        at = pl.ds(pl.multiple_of(jnp.clip(there, 0, groups - 1) * span, span), span)
        parts.append(heater[:, at] * inside)
    near = jnp.concatenate(parts, axis=1).astype(F32)
    near = jnp.where(even, jnp.concatenate([near[1:], near[:1]], axis=0), near)
    near = jnp.concatenate([near, jnp.zeros((SIDE - 2, 3 * span), F32)], axis=0).astype(BF16)
    row, lane = iota((span + SIDE, 3 * span), 0), iota((span + SIDE, 3 * span), 1)
    pick = one_hot(lane == jnp.where(row < span + SIDE // 2, span + row, row - SIDE))
    heat[...] = lax.dot_general(pick, near, (((1,), (1,)), ((), ())), preferred_element_type=F32)
    together = 4
    wide = together * modes
    for first in range(0, groups, together):
        lanes = pl.ds(first // together * wide, wide)
        members = range(first, first + together)
        edge = jnp.concatenate([received[j, modes:, :modes] for j in members], axis=1).astype(F32)
        vector = jnp.concatenate(
            [received[j, modes:, span : span + modes] for j in members], axis=1
        ).astype(F32)
        vector = vector + pltpu.roll(vector, 4, 0)
        sign = jnp.where((iota((SIDE, wide), 0) == 0) & jnp.logical_not(even), -1.0, 1.0)
        coef[:, lanes] = vector * sign
        other = pltpu.roll(edge, 4, 0)
        for c, out in ((0, own_0), (1, own_1)):
            column = jnp.where(even, 1 - c, c)
            at = pl.ds(pl.multiple_of(column * span, span), span)
            block = jnp.concatenate([received[j, :modes, at] for j in members], axis=0)
            turned = lax.dot_general(
                unit, block, (((1,), (1,)), ((), ())), preferred_element_type=F32
            )
            ends = jnp.where(column == 0, edge, other)
            out[:, lanes] = jnp.concatenate([turned, ends], axis=0).astype(BF16)


def unpack(received, heater):
    groups, height, cells = received.shape
    total, rows = groups * (height - SIDE), cells // 2 + SIDE
    return pl.pallas_call(
        unpack_body,
        in_specs=[IN_VMEM] * 2,
        out_specs=[IN_VMEM] * 4,
        out_shape=[jax.ShapeDtypeStruct((rows, total), BF16)] * 2
        + [jax.ShapeDtypeStruct((SIDE, total), F32), jax.ShapeDtypeStruct((rows, SIDE), F32)],
        compiler_params=params(24),
        cost_estimate=pl.CostEstimate(flops=10**7, bytes_accessed=3 * MIB, transcendentals=0),
        name="unpack",
    )(received, heater)


def scatter(matrix, values):
    return lax.dot_general(
        values, matrix, (((1,), (1,)), ((), ())), preferred_element_type=F32
    )


def local_terms(scattered, mine, other, x_rate, coef, heat):
    rows, kept = mine.shape[0], scattered.shape[0]
    y_rate, inverse, emit = (coef[k : k + 1, :] for k in (1, 2, 3))
    return (
        scattered * inverse
        + heat * emit
        + jnp.maximum(y_rate, 0.0) * pltpu.roll(mine, 1, 0)[:kept]
        + jnp.maximum(-y_rate, 0.0) * pltpu.roll(mine, rows - 1, 0)[:kept]
        + x_rate * other[:kept]
    )


def first_body(own_0, own_1, matrix, coef, heat, part_0, part_1, sent_0, sent_1, both):
    rows, total = own_0.shape
    span = rows - SIDE
    both[:rows, :] = own_0[...].astype(F32).astype(BF16)
    both[rows:, :] = own_1[...].astype(F32).astype(BF16)
    for first in range(0, total, TILE):
        at = pl.ds(first, TILE)
        x_rate = coef[0:1, at]
        wide_0, wide_1 = own_0[:, at].astype(F32), own_1[:, at].astype(F32)
        scattered = scatter(matrix[at, :], both[...])
        value = local_terms(
            scattered[:rows], wide_0, wide_1, jnp.maximum(x_rate, 0.0), coef[:, at], heat[:, 0:1]
        )
        part_0[:, at] = value
        sent_0[:, at] = value[:span].astype(BF16)
        value = local_terms(
            scattered[rows:], wide_1, wide_0, jnp.maximum(-x_rate, 0.0), coef[:, at], heat[:, 1:2]
        )
        part_1[:, at] = value
        sent_1[:, at] = value[:span].astype(BF16)


def first_step(own_0, own_1, matrix, coef, heat):
    rows, total = own_0.shape
    return pl.pallas_call(
        first_body,
        in_specs=[IN_VMEM] * 5,
        out_specs=[IN_VMEM] * 4,
        out_shape=[jax.ShapeDtypeStruct((rows, total), F32)] * 2
        + [jax.ShapeDtypeStruct((rows - SIDE, total), BF16)] * 2,
        scratch_shapes=[pltpu.VMEM((2 * rows, total), BF16)],
        compiler_params=params(24),
        cost_estimate=pl.CostEstimate(
            flops=4 * rows * total * total, bytes_accessed=8 * MIB, transcendentals=0
        ),
        name="first_step",
    )(own_0, own_1, matrix, coef, heat)


def second_body(part_0, part_1, near_0, near_1, matrix, coef, heat, base_0, base_1, field, narrow):
    span, total = base_0.shape
    x_rate = coef[0:1, :]
    field[0] = part_0[...] + jnp.maximum(-x_rate, 0.0) * near_0[...].astype(F32)
    field[1] = part_1[...] + jnp.maximum(x_rate, 0.0) * near_1[...].astype(F32)
    for c in range(2):
        narrow[c * span : (c + 1) * span, :] = field[c, :span, :].astype(BF16)
    for first in range(0, total, TILE):
        at = pl.ds(first, TILE)
        x_rate = coef[0:1, at]
        scattered = scatter(matrix[at, :], narrow[...])
        mine_0, mine_1 = field[0, :, at], field[1, :, at]
        base_0[:, at] = local_terms(
            scattered[:span], mine_0, mine_1, jnp.maximum(x_rate, 0.0), coef[:, at], heat[:span, 0:1]
        )
        base_1[:, at] = local_terms(
            scattered[span:], mine_1, mine_0, jnp.maximum(-x_rate, 0.0), coef[:, at], heat[:span, 1:2]
        )


def second_step(part_0, part_1, near_0, near_1, matrix, coef, heat):
    rows, total = part_0.shape
    span = rows - SIDE
    return pl.pallas_call(
        second_body,
        in_specs=[IN_VMEM] * 7,
        out_specs=[IN_VMEM] * 2,
        out_shape=[jax.ShapeDtypeStruct((span, total), F32)] * 2,
        scratch_shapes=[pltpu.VMEM((2, rows, total), F32), pltpu.VMEM((2 * span, total), BF16)],
        compiler_params=params(24),
        cost_estimate=pl.CostEstimate(
            flops=4 * rows * total * total, bytes_accessed=8 * MIB, transcendentals=0
        ),
        name="second_step",
    )(part_0, part_1, near_0, near_1, matrix, coef, heat)


def finish_body(base_0, base_1, near_0, near_1, coef, result):
    groups, modes, cells = result.shape
    even = lax.axis_index("cell") % 2 == 0
    span = cells // 2
    unit = one_hot(iota((span, span), 0) == iota((span, span), 1))
    together = 4
    wide = together * modes
    for first in range(0, groups, together):
        lanes = pl.ds(first // together * wide, wide)
        x_rate = coef[0:1, lanes]
        for c, base, outer, rate in (
            (0, base_0, near_0, jnp.maximum(-x_rate, 0.0)),
            (1, base_1, near_1, jnp.maximum(x_rate, 0.0)),
        ):
            at = pl.ds(pl.multiple_of(jnp.where(even, 1 - c, c) * span, span), span)
            value = base[:, lanes] + rate * outer[:, lanes].astype(F32)
            turned = lax.dot_general(
                value.astype(BF16), unit, (((0,), (0,)), ((), ())), preferred_element_type=F32
            ).astype(BF16)
            for k in range(together):
                result[first + k, :, at] = turned[k * modes : (k + 1) * modes]


def finish(base_0, base_1, near_0, near_1, coef, groups):
    span, total = base_0.shape
    return pl.pallas_call(
        finish_body,
        out_shape=jax.ShapeDtypeStruct((groups, total // groups, 2 * span), BF16),
        compiler_params=params(32),
        cost_estimate=pl.CostEstimate(flops=10**7, bytes_accessed=3 * MIB, transcendentals=0),
        name="finish",
    )(base_0, base_1, near_0, near_1, coef)


def spread_body(result, out, wide, sent):
    groups, modes, cells = result.shape
    span, per = cells // 2, groups // PIECES
    row, lane = iota((2 * modes, 2 * modes), 0), iota((2 * modes, 2 * modes), 1)
    join = one_hot(row == jnp.where(lane < modes, 2 * lane, 2 * (lane - modes) + 1))
    copies = []
    for k in range(PIECES):
        for group in range(k * per, (k + 1) * per):
            both = jnp.concatenate([result[group, :, :span], result[group, :, span:]], axis=0)
            both = jnp.dot(join, both, preferred_element_type=F32)
            wide[:, :, pl.ds(group * span, span)] = both.reshape(modes, 2, span)
        at = pl.ds(k * per * span, per * span)
        copies.append(pltpu.make_async_copy(wide.at[:, :, at], out.at[:, :, at], sent.at[k]))
        copies[-1].start()
    for copy in copies:
        copy.wait()


def spread(result, cols):
    groups, modes, cells = result.shape
    shape = (modes, cols, groups * cells // cols)
    return pl.pallas_call(
        spread_body,
        in_specs=[IN_VMEM],
        out_specs=IN_HBM,
        out_shape=jax.ShapeDtypeStruct(shape, F32),
        scratch_shapes=[pltpu.VMEM(shape, F32), pltpu.SemaphoreType.DMA((PIECES,))],
        compiler_params=params(24),
        cost_estimate=pl.CostEstimate(flops=10**7, bytes_accessed=3 * MIB, transcendentals=0),
        name="spread",
    )(result)


def shards(initial, scatter_matrix, speed_x, speed_y, relaxation, emission, heater):
    modes, cols, length = initial.shape
    groups = lax.axis_size("mode")
    span = length // groups

    packed = pack(initial, (speed_x, speed_y, relaxation, emission), groups)
    received = lax.all_to_all(packed, "mode", 0, 0, tiled=True)
    own_0, own_1, coef, heat = unpack(received, heater)
    near_0, near_1 = swap(own_0, own_1)
    part_0, part_1, sent_0, sent_1 = first_step(own_0, own_1, scatter_matrix, coef, heat)
    far_0, far_1 = swap(sent_0, sent_1)
    base_0, base_1 = second_step(part_0, part_1, near_0, near_1, scatter_matrix, coef, heat)
    result = finish(base_0, base_1, far_0, far_1, coef, groups)
    result = lax.all_to_all(result, "mode", 0, 0, tiled=True)
    return spread(result, cols)


def solution(mesh):
    return jax.shard_map(
        shards,
        mesh=mesh,
        in_specs=(
            P("mode", "cell", None),
            P(),
            P("mode"),
            P("mode"),
            P("mode"),
            P("mode"),
            P("cell", None),
        ),
        out_specs=P("mode", "cell", None),
        check_vma=False,
    )
```

time: 100 us -> 95.2 us (0.952)
  blocking collectives: 27.1 us -> 58.4 us
  waiting for transfers between devices: 27.5 us -> 10.1 us
  local copies, waits for them, and re-layouts: 16.2 us -> 2.34 us
  starting transfers between devices: 21.7 us -> 14.2 us
  Pallas kernels: 6.99 us -> 9.64 us
    all_to_all x1 -> x2, blocking collectives: 27.1 us -> 58.4 us  [the longest x1 32.1 us: shards(): received = lax.all_to_all(packed, 'mode', 0, 0, tiled=True)]
    all_to_all x1 -> x0, waiting for transfers between devices: 16.8 us -> none  [shards(): received = lax.all_to_all(packed, 'mode', 0, 0, tiled=True)]
    unnamed x17 -> x6, local copies, waits for them, and re-layouts: 13 us -> 2.34 us
    all_to_all x1 -> x0, starting transfers between devices: 7.8 us -> none  [shards(): received = lax.all_to_all(packed, 'mode', 0, 0, tiled=True)]
    convert_element_type x2 -> x0, local copies, waits for them, and re-layouts: 2.8 us -> none  [shards(): return out.reshape(modes, cols, length).astype(F32)]
    pallas_call x1 -> x2, Pallas kernels: 0.46 us -> 1.95 us  [the longest x1 1.45 us: spread(): pl.pallas_call(spread_body, in_specs=[IN_VMEM], out_specs=IN_HBM, out_sha...]
  transfers between devices with their start and end apart: 5 -> 4, of which waited for: 3 -> 3; matrix products, arithmetic and copies ran while one was open for 7% -> 0% of each run, Pallas kernels for 4% -> 4%
where the time goes in v4:
time: 95.2 us; the launch traced here: 94.8 us
  blocking collectives  58.4 us (61%)
  starting transfers between devices  14.2 us (15%)
  waiting for transfers between devices  10.1 us (11%)
  Pallas kernels  9.64 us (10%)
  local copies, waits for them, and re-layouts  2.34 us (2%)
    all_to_all x1, blocking collectives, shards(): received = lax.all_to_all(packed, 'mode', 0, 0, tiled=True)  32.1 us
    all_to_all x1, blocking collectives, shards(): result = lax.all_to_all(result, 'mode', 0, 0, tiled=True)  26.3 us
    ppermute x2, starting transfers between devices, swap(): lax.ppermute(to_second, 'cell', inside(second))  9.81 us
    ppermute x2, waiting for transfers between devices, swap(): lax.ppermute(to_second, 'cell', inside(second))  5.9 us
    ppermute x2, starting transfers between devices, swap(): lax.ppermute(to_first, 'cell', inside(first))  4.38 us
    ppermute x2, waiting for transfers between devices, swap(): lax.ppermute(to_first, 'cell', inside(first))  4.25 us
    pallas_call x1, Pallas kernels, pack(): pl.pallas_call(pack_body, in_specs=[IN_HBM] * 5, out_specs=IN_VMEM, scrat...  3.37 us
    unnamed x6, local copies, waits for them, and re-layouts  2.34 us
  transfers between devices with their start and end apart: 4, of which 3 were waited for; matrix products, arithmetic and copies ran while one was open for 0% of the time, Pallas kernels for 4%

profile of v4, /device:TPU:199, one launch (start us, length us, event | category | flops | bytes accessed | tf_op | source)
XLA Modules:
  0.0 94.8 jit_solution(10166326377899347499)
XLA Ops:
  0.0 0.0 copy-start.2
  0.0 3.4 %pack.1 = bf16[16,104,256]{2,1,0:T(8,128)(2,1)} custom-call(f32[1,96]{1,0:T(1,128)} %bitcast.4, f32[1,96]{1,0:T(1,128)} %bitcast.5, f32[1,96]{1,0:T(1,128)} %bitcast.6, f32[1,96]{1,0:T(1,128)} %bitcast.7, f32[96,2,2048]{2,1,0:T(2,128)} %initial_in.1), custom_call_target="tpu_custom_call" | custom-call | flops 10000000 | bytes 3145728 | tf_op jit(solution)/shard_map/pack/pallas_call | solution.py:104
  3.4 32.1 %all_to_all.10.received = bf16[16,104,256]{2,1,0:T(8,128)(2,1)S(1)} all-to-all(bf16[16,104,256]{2,1,0:T(8,128)(2,1)} %pack.1), channel_id=1, replica_groups=mesh['mode'=16,'cell'=32] {'mode'}, dimensions={0} | all-to-all | bytes 1703936 | tf_op jit(solution)/shard_map/all_to_all | solution.py:341
  35.5 0.0 copy-done.2
  35.5 0.5 unpack.1
  36.0 2.5 %collective-permute-start = (bf16[136,1536]{1,0:T(8,128)(2,1)S(1)}, bf16[136,1536]{1,0:T(8,128)(2,1)S(1)}, u32[]{:S(2)}, u32[]{:S(2)}) collective-permute-start(bf16[136,1536]{1,0:T(8,128)(2,1)S(1)} %get-tuple-element.15.own_0), channel_id=1, source_target_pairs={{0,1},{1,0},{2,3},{3,2},{4,5},{5,4},{6,7},{7,6},{8,9},{9,8},{10,11... | collective-permute-start | bytes 1253384 | tf_op jit(solution)/shard_map/ppermute | solution.py:23
  38.5 5.8 %collective-permute-start.1 = (bf16[136,1536]{1,0:T(8,128)(2,1)S(1)}, bf16[136,1536]{1,0:T(8,128)(2,1)S(1)}, u32[]{:S(2)}, u32[]{:S(2)}) collective-permute-start(bf16[136,1536]{1,0:T(8,128)(2,1)S(1)} %get-tuple-element.16.own_1), channel_id=1, source_target_pairs={{1,2},{2,1},{3,4},{4,3},{5,6},{6,5},{7,8},{8,7},{9,10},{10,9},{11,... | collective-permute-start | bytes 1253384 | tf_op jit(solution)/shard_map/ppermute | solution.py:24
  44.3 0.0 copy-start
  44.3 2.3 %copy-done = bf16[1536,1536]{1,0:T(8,128)(2,1)S(1)} copy-done((bf16[1536,1536]{1,0:T(8,128)(2,1)S(1)}, bf16[1536,1536]{1,0:T(8,128)(2,1)}, u32[]{:S(2)}) %copy-start) | copy-done | bytes 4718616
  46.6 0.0 copy-start.1
  46.6 2.0 %first_step.1 = (f32[136,1536]{1,0:T(8,128)S(1)}, f32[136,1536]{1,0:T(8,128)S(1)}, bf16[128,1536]{1,0:T(8,128)(2,1)S(1)}, bf16[128,1536]{1,0:T(8,128)(2,1)S(1)}) custom-call(bf16[136,1536]{1,0:T(8,128)(2,1)S(1)} %get-tuple-element.15.own_0, bf16[136,1536]{1,0:T(8,128)(2,1)S(1)} %get-tuple-element.16.own_1, bf16[1536,1536]{1,0:T(8,128)(2,1)S(1)} %copy-done, ...), custom_call_target="tpu_custom_call" | custom-call | flops 1283457024 | bytes 8388608 | tf_op jit(solution)/shard_map/first_step/pallas_call | solution.py:216
  48.7 1.9 %collective-permute-start.2 = (bf16[128,1536]{1,0:T(8,128)(2,1)S(1)}, bf16[128,1536]{1,0:T(8,128)(2,1)S(1)}, u32[]{:S(2)}, u32[]{:S(2)}) collective-permute-start(bf16[128,1536]{1,0:T(8,128)(2,1)S(1)} %get-tuple-element.23), channel_id=1, source_target_pairs={{0,1},{1,0},{2,3},{3,2},{4,5},{5,4},{6,7},{7,6},{8,9},{9,8},{10,11... | collective-permute-start | bytes 1179656 | tf_op jit(solution)/shard_map/ppermute | solution.py:23
  50.6 4.0 %collective-permute-start.3 = (bf16[128,1536]{1,0:T(8,128)(2,1)S(1)}, bf16[128,1536]{1,0:T(8,128)(2,1)S(1)}, u32[]{:S(2)}, u32[]{:S(2)}) collective-permute-start(bf16[128,1536]{1,0:T(8,128)(2,1)S(1)} %get-tuple-element.24), channel_id=1, source_target_pairs={{1,2},{2,1},{3,4},{4,3},{5,6},{6,5},{7,8},{8,7},{9,10},{10,9},{11,... | collective-permute-start | bytes 1179656 | tf_op jit(solution)/shard_map/ppermute | solution.py:24
  54.6 0.0 collective-permute-done.near_0
  54.6 0.6 collective-permute-done.1.near_1
  55.3 0.0 copy-done.1
  55.3 1.9 %second_step.1 = (f32[128,1536]{1,0:T(8,128)S(1)}, f32[128,1536]{1,0:T(8,128)S(1)}) custom-call(f32[136,1536]{1,0:T(8,128)S(1)} %get-tuple-element.19.part_0, f32[136,1536]{1,0:T(8,128)S(1)} %get-tuple-element.20.part_1, bf16[136,1536]{1,0:T(8,128)(2,1)S(1)} %collective-permute-done.near_0, bf16[136,1536]{1,0:T(8,128)(2,1)S(1)} %collective-permute-done.1.near_1, ...), custom_call_target="tpu_custom_call" | custom-call | flops 1283457024 | bytes 8388608 | tf_op jit(solution)/shard_map/second_step/pallas_call | solution.py:254
  57.2 4.2 %collective-permute-done.2.near_0 = bf16[128,1536]{1,0:T(8,128)(2,1)S(1)} collective-permute-done((bf16[128,1536]{1,0:T(8,128)(2,1)S(1)}, bf16[128,1536]{1,0:T(8,128)(2,1)S(1)}, u32[]{:S(2)}, u32[]{:S(2)}) %collective-permute-start.2) | collective-permute-done | bytes 393248 | tf_op jit(solution)/shard_map/ppermute | solution.py:23
  61.4 5.2 %collective-permute-done.3.near_1 = bf16[128,1536]{1,0:T(8,128)(2,1)S(1)} collective-permute-done((bf16[128,1536]{1,0:T(8,128)(2,1)S(1)}, bf16[128,1536]{1,0:T(8,128)(2,1)S(1)}, u32[]{:S(2)}, u32[]{:S(2)}) %collective-permute-start.3) | collective-permute-done | bytes 393248 | tf_op jit(solution)/shard_map/ppermute | solution.py:24
  66.7 0.4 finish.1
  67.1 26.3 %all_to_all.11.result = bf16[16,96,256]{2,1,0:T(8,128)(2,1)S(1)} all-to-all(bf16[16,96,256]{2,1,0:T(8,128)(2,1)S(1)} %finish.1), channel_id=1, replica_groups=mesh['mode'=16,'cell'=32] {'mode'}, dimensions={0} | all-to-all | bytes 1572864 | tf_op jit(solution)/shard_map/all_to_all | solution.py:348
  93.4 1.5 %spread.1 = f32[96,2,2048]{2,1,0:T(2,128)} custom-call(bf16[16,96,256]{2,1,0:T(8,128)(2,1)S(1)} %all_to_all.11.result), custom_call_target="tpu_custom_call" | custom-call | flops 10000000 | bytes 3145728 | tf_op jit(solution)/shard_map/spread/pallas_call | solution.py:323
Async XLA Ops:
  0.0 35.5 %copy-start.2 = (s32[2,2048]{1,0:T(2,128)S(1)}, s32[2,2048]{1,0:T(2,128)}, u32[]{:S(2)}) copy-start(s32[2,2048]{1,0:T(2,128)} %heater.1) | copy-start | bytes 49156
  36.0 18.6 %collective-permute-start = (bf16[136,1536]{1,0:T(8,128)(2,1)S(1)}, bf16[136,1536]{1,0:T(8,128)(2,1)S(1)}, u32[]{:S(2)}, u32[]{:S(2)}) collective-permute-start(bf16[136,1536]{1,0:T(8,128)(2,1)S(1)} %get-tuple-element.15.own_0), channel_id=1, source_target_pairs={{0,1},{1,0},{2,3},{3,2},{4,5},{5,4},{6,7},{7,6},{8,9},{9,8},{10,11... | collective-permute-start | bytes 1253384 | tf_op jit(solution)/shard_map/ppermute | solution.py:23
  38.5 16.8 %collective-permute-start.1 = (bf16[136,1536]{1,0:T(8,128)(2,1)S(1)}, bf16[136,1536]{1,0:T(8,128)(2,1)S(1)}, u32[]{:S(2)}, u32[]{:S(2)}) collective-permute-start(bf16[136,1536]{1,0:T(8,128)(2,1)S(1)} %get-tuple-element.16.own_1), channel_id=1, source_target_pairs={{1,2},{2,1},{3,4},{4,3},{5,6},{6,5},{7,8},{8,7},{9,10},{10,9},{11,... | collective-permute-start | bytes 1253384 | tf_op jit(solution)/shard_map/ppermute | solution.py:24
  44.3 2.3 %copy-start = (bf16[1536,1536]{1,0:T(8,128)(2,1)S(1)}, bf16[1536,1536]{1,0:T(8,128)(2,1)}, u32[]{:S(2)}) copy-start(bf16[1536,1536]{1,0:T(8,128)(2,1)} %matrix.3) | copy-start | bytes 14155780
  46.6 8.6 %copy-start.1 = (bf16[1536,1536]{1,0:T(8,128)(2,1)S(1)}, bf16[1536,1536]{1,0:T(8,128)(2,1)}, u32[]{:S(2)}) copy-start(bf16[1536,1536]{1,0:T(8,128)(2,1)} %matrix.3) | copy-start | bytes 14155780
  48.7 12.8 %collective-permute-start.2 = (bf16[128,1536]{1,0:T(8,128)(2,1)S(1)}, bf16[128,1536]{1,0:T(8,128)(2,1)S(1)}, u32[]{:S(2)}, u32[]{:S(2)}) collective-permute-start(bf16[128,1536]{1,0:T(8,128)(2,1)S(1)} %get-tuple-element.23), channel_id=1, source_target_pairs={{0,1},{1,0},{2,3},{3,2},{4,5},{5,4},{6,7},{7,6},{8,9},{9,8},{10,11... | collective-permute-start | bytes 1179656 | tf_op jit(solution)/shard_map/ppermute | solution.py:23
  50.6 16.1 %collective-permute-start.3 = (bf16[128,1536]{1,0:T(8,128)(2,1)S(1)}, bf16[128,1536]{1,0:T(8,128)(2,1)S(1)}, u32[]{:S(2)}, u32[]{:S(2)}) collective-permute-start(bf16[128,1536]{1,0:T(8,128)(2,1)S(1)} %get-tuple-element.24), channel_id=1, source_target_pairs={{1,2},{2,1},{3,4},{4,3},{5,6},{6,5},{7,8},{8,7},{9,10},{10,9},{11,... | collective-permute-start | bytes 1179656 | tf_op jit(solution)/shard_map/ppermute | solution.py:24

commit v5 on v4

--- a/solution.py
+++ b/solution.py
@@ -11,7 +11,6 @@
 TILE = 256
 MIB = 1024 * 1024
 PIECES = 4
-PACK_LIMIT = 62
 
 
 def swap(to_first, to_second):
@@ -41,23 +40,10 @@
     return lax.broadcasted_iota(jnp.int32, shape, axis)
 
 
-def pack_body(
-    speed_x_in, speed_y_in, relaxation_in, emission_in, initial_in, packed,
-    speed_x, speed_y, relaxation, emission, initial, arrived,
-):
+def pack_body(rates, initial, packed):
     groups, height, cells = packed.shape
     modes, span = height - SIDE, cells // 2
     per = groups // PIECES
-    pairs = ((speed_x_in, speed_x), (speed_y_in, speed_y), (relaxation_in, relaxation), (emission_in, emission))
-    small = [pltpu.make_async_copy(*pair, arrived.at[k]) for k, pair in enumerate(pairs)]
-    large = []
-    for k in range(PIECES):
-        at = pl.ds(k * per * span, per * span)
-        large.append(
-            pltpu.make_async_copy(initial_in.at[:, :, at], initial.at[:, :, at], arrived.at[4 + k])
-        )
-    for copy in large[:1] + small + large[1:]:
-        copy.start()
     wide = 2 * modes
     row, lane = iota((wide, wide), 0), iota((wide, wide), 1)
     apart = one_hot(lane == jnp.where(row < modes, 2 * row, 2 * (row - modes) + 1))
@@ -66,7 +52,6 @@
     target = lane // SIDE * span + lane % 2 + jnp.where(after, span, -2) - row
     ends = jnp.zeros((wide, groups * SIDE), F32)
     for k in range(PIECES):
-        large[k].wait()
         first = k * per * span
         both = [
             initial[:, :, pl.ds(first + g * span, span)].reshape(wide, span).astype(BF16)
@@ -85,11 +70,9 @@
     ).T
     middle = (iota((groups * SIDE, span), 0) % SIDE) // 2
     ends = jnp.where((middle == 1) | (middle == 2), ends[:, span:], ends[:, :span])
-    for copy in small:
-        copy.wait()
-    sx, sy = speed_x[...], speed_y[...]
-    inverse = 1.0 / (relaxation[...] + jnp.abs(sx) + jnp.abs(sy))
-    vectors = jnp.concatenate([sx * inverse, sy * inverse, inverse, emission[...] * inverse], axis=0)
+    sx, sy, relaxation, emission = (rates[k : k + 1, :] for k in range(4))
+    inverse = 1.0 / (relaxation + jnp.abs(sx) + jnp.abs(sy))
+    vectors = jnp.concatenate([sx * inverse, sy * inverse, inverse, emission * inverse], axis=0)
     high = vectors.astype(BF16).astype(F32)
     vectors = jnp.concatenate([high, vectors - high], axis=0)
     vectors = jnp.concatenate([vectors, jnp.zeros((SIDE, span - modes), F32)], axis=1)
@@ -98,40 +81,25 @@
         packed[group, modes:, :] = jnp.concatenate([edge, vectors], axis=1).astype(BF16)
 
 
-def pack(initial, vectors, groups):
+def pack(initial, rates, groups):
     modes, cols, length = initial.shape
     shape = (groups, modes + SIDE, cols * length // groups)
     return pl.pallas_call(
         pack_body,
-        in_specs=[IN_HBM] * 5,
+        in_specs=[IN_VMEM] * 2,
         out_specs=IN_VMEM,
-        scratch_shapes=[pltpu.VMEM((1, modes), F32)] * 4
-        + [pltpu.VMEM(initial.shape, F32), pltpu.SemaphoreType.DMA((4 + PIECES,))],
         out_shape=jax.ShapeDtypeStruct(shape, BF16),
-        compiler_params=params(PACK_LIMIT),
+        compiler_params=params(24),
         cost_estimate=pl.CostEstimate(flops=10**7, bytes_accessed=3 * MIB, transcendentals=0),
         name="pack",
-    )(*[v[None] for v in vectors], initial)
-
-
-def unpack_body(received, heater, own_0, own_1, coef, heat):
+    )(rates, initial)
+
+
+def unpack_body(received, own_0, own_1, coef):
     groups, height, cells = received.shape
     modes, span = height - SIDE, cells // 2
     unit = one_hot(iota((span, span), 0) == iota((span, span), 1))
-    me = lax.axis_index("mode")
     even = lax.axis_index("cell") % 2 == 0
-    parts = []
-    for k in (-1, 0, 1):
-        there = me + k
-        inside = ((there >= 0) & (there < groups)).astype(jnp.int32)
-        at = pl.ds(pl.multiple_of(jnp.clip(there, 0, groups - 1) * span, span), span)
-        parts.append(heater[:, at] * inside)
-    near = jnp.concatenate(parts, axis=1).astype(F32)
-    near = jnp.where(even, jnp.concatenate([near[1:], near[:1]], axis=0), near)
-    near = jnp.concatenate([near, jnp.zeros((SIDE - 2, 3 * span), F32)], axis=0).astype(BF16)
-    row, lane = iota((span + SIDE, 3 * span), 0), iota((span + SIDE, 3 * span), 1)
-    pick = one_hot(lane == jnp.where(row < span + SIDE // 2, span + row, row - SIDE))
-    heat[...] = lax.dot_general(pick, near, (((1,), (1,)), ((), ())), preferred_element_type=F32)
     together = 4
     wide = together * modes
     for first in range(0, groups, together):
@@ -156,19 +124,19 @@
             out[:, lanes] = jnp.concatenate([turned, ends], axis=0).astype(BF16)
 
 
-def unpack(received, heater):
+def unpack(received):
     groups, height, cells = received.shape
     total, rows = groups * (height - SIDE), cells // 2 + SIDE
     return pl.pallas_call(
         unpack_body,
-        in_specs=[IN_VMEM] * 2,
-        out_specs=[IN_VMEM] * 4,
+        in_specs=[IN_VMEM],
+        out_specs=[IN_VMEM] * 3,
         out_shape=[jax.ShapeDtypeStruct((rows, total), BF16)] * 2
-        + [jax.ShapeDtypeStruct((SIDE, total), F32), jax.ShapeDtypeStruct((rows, SIDE), F32)],
+        + [jax.ShapeDtypeStruct((SIDE, total), F32)],
         compiler_params=params(24),
         cost_estimate=pl.CostEstimate(flops=10**7, bytes_accessed=3 * MIB, transcendentals=0),
         name="unpack",
-    )(received, heater)
+    )(received)
 
 
 def scatter(matrix, values):
@@ -189,9 +157,24 @@
     )
 
 
-def first_body(own_0, own_1, matrix, coef, heat, part_0, part_1, sent_0, sent_1, both):
+def first_body(own_0, own_1, matrix, coef, heater, part_0, part_1, sent_0, sent_1, heat, both):
     rows, total = own_0.shape
     span = rows - SIDE
+    groups = heater.shape[1] // span
+    me = lax.axis_index("mode")
+    even = lax.axis_index("cell") % 2 == 0
+    parts = []
+    for k in (-1, 0, 1):
+        there = me + k
+        inside = ((there >= 0) & (there < groups)).astype(jnp.int32)
+        at = pl.ds(pl.multiple_of(jnp.clip(there, 0, groups - 1) * span, span), span)
+        parts.append(heater[:, at] * inside)
+    near = jnp.concatenate(parts, axis=1).astype(F32)
+    near = jnp.where(even, jnp.concatenate([near[1:], near[:1]], axis=0), near)
+    near = jnp.concatenate([near, jnp.zeros((SIDE - 2, 3 * span), F32)], axis=0).astype(BF16)
+    row, lane = iota((span + SIDE, 3 * span), 0), iota((span + SIDE, 3 * span), 1)
+    pick = one_hot(lane == jnp.where(row < span + SIDE // 2, span + row, row - SIDE))
+    heat[...] = lax.dot_general(pick, near, (((1,), (1,)), ((), ())), preferred_element_type=F32)
     both[:rows, :] = own_0[...].astype(F32).astype(BF16)
     both[rows:, :] = own_1[...].astype(F32).astype(BF16)
     for first in range(0, total, TILE):
@@ -211,21 +194,22 @@
         sent_1[:, at] = value[:span].astype(BF16)
 
 
-def first_step(own_0, own_1, matrix, coef, heat):
+def first_step(own_0, own_1, matrix, coef, heater):
     rows, total = own_0.shape
     return pl.pallas_call(
         first_body,
         in_specs=[IN_VMEM] * 5,
-        out_specs=[IN_VMEM] * 4,
+        out_specs=[IN_VMEM] * 5,
         out_shape=[jax.ShapeDtypeStruct((rows, total), F32)] * 2
-        + [jax.ShapeDtypeStruct((rows - SIDE, total), BF16)] * 2,
+        + [jax.ShapeDtypeStruct((rows - SIDE, total), BF16)] * 2
+        + [jax.ShapeDtypeStruct((rows, SIDE), F32)],
         scratch_shapes=[pltpu.VMEM((2 * rows, total), BF16)],
         compiler_params=params(24),
         cost_estimate=pl.CostEstimate(
             flops=4 * rows * total * total, bytes_accessed=8 * MIB, transcendentals=0
         ),
         name="first_step",
-    )(own_0, own_1, matrix, coef, heat)
+    )(own_0, own_1, matrix, coef, heater)
 
 
 def second_body(part_0, part_1, near_0, near_1, matrix, coef, heat, base_0, base_1, field, narrow):
@@ -337,11 +321,11 @@
     groups = lax.axis_size("mode")
     span = length // groups
 
-    packed = pack(initial, (speed_x, speed_y, relaxation, emission), groups)
+    packed = pack(initial, jnp.stack([speed_x, speed_y, relaxation, emission]), groups)
     received = lax.all_to_all(packed, "mode", 0, 0, tiled=True)
-    own_0, own_1, coef, heat = unpack(received, heater)
+    own_0, own_1, coef = unpack(received)
     near_0, near_1 = swap(own_0, own_1)
-    part_0, part_1, sent_0, sent_1 = first_step(own_0, own_1, scatter_matrix, coef, heat)
+    part_0, part_1, sent_0, sent_1, heat = first_step(own_0, own_1, scatter_matrix, coef, heater)
     far_0, far_1 = swap(sent_0, sent_1)
     base_0, base_1 = second_step(part_0, part_1, near_0, near_1, scatter_matrix, coef, heat)
     result = finish(base_0, base_1, far_0, far_1, coef, groups)

time: 95.2 us -> 92.4 us (0.971)
  Pallas kernels: 9.64 us -> 7.33 us
    pallas_call x2, Pallas kernels: 3.87 us -> 1.42 us  [the longest x1 0.95 us: pack(): pl.pallas_call(pack_body, in_specs=[IN_VMEM] * 2, out_specs=IN_VMEM, out_...]
    ppermute x2, waiting for transfers between devices: 4.25 us -> 1.96 us  [swap(): lax.ppermute(to_first, 'cell', inside(first))]
    ppermute x2, waiting for transfers between devices: 5.9 us -> 8.12 us  [swap(): lax.ppermute(to_second, 'cell', inside(second))]
where the time goes in v5:
time: 92.4 us; the launch traced here: 92.2 us
  blocking collectives  58.3 us (63%)
  starting transfers between devices  14.2 us (15%)
  waiting for transfers between devices  10.1 us (11%)
  Pallas kernels  7.33 us (8%)
  local copies, waits for them, and re-layouts  1.41 us (2%)
    all_to_all x1, blocking collectives, shards(): received = lax.all_to_all(packed, 'mode', 0, 0, tiled=True)  32.1 us
    all_to_all x1, blocking collectives, shards(): result = lax.all_to_all(result, 'mode', 0, 0, tiled=True)  26.3 us
    ppermute x2, starting transfers between devices, swap(): lax.ppermute(to_second, 'cell', inside(second))  9.82 us
    ppermute x2, waiting for transfers between devices, swap(): lax.ppermute(to_second, 'cell', inside(second))  8.12 us
    ppermute x2, starting transfers between devices, swap(): lax.ppermute(to_first, 'cell', inside(first))  4.38 us
    pallas_call x1, Pallas kernels, first_step(): pl.pallas_call(first_body, in_specs=[IN_VMEM] * 5, out_specs=[IN_VMEM] *...  2.11 us
    ppermute x2, waiting for transfers between devices, swap(): lax.ppermute(to_first, 'cell', inside(first))  1.96 us
    pallas_call x1, Pallas kernels, second_step(): pl.pallas_call(second_body, in_specs=[IN_VMEM] * 7, out_specs=[IN_VMEM] *...  1.92 us
  transfers between devices with their start and end apart: 4, of which 3 were waited for; matrix products, arithmetic and copies ran while one was open for 0% of the time, Pallas kernels for 4%

profile of v5, /device:TPU:199, one launch (start us, length us, event | category | flops | bytes accessed | tf_op | source)
XLA Modules:
  0.0 92.2 jit_solution(6377274266862221153)
XLA Ops:
  0.0 0.7 pad_maximum_fusion.rates
  0.7 0.0 copy-start.1
  0.7 1.4 %copy-done.1 = f32[96,2,2048]{2,1,0:T(2,128)S(1)} copy-done((f32[96,2,2048]{2,1,0:T(2,128)S(1)}, f32[96,2,2048]{2,1,0:T(2,128)}, u32[]{:S(2)}) %copy-start.1) | copy-done | bytes 1572888
  2.1 0.0 copy-start
  2.1 0.9 %pack.1 = bf16[16,104,256]{2,1,0:T(8,128)(2,1)S(1)} custom-call(f32[4,96]{1,0:T(4,128)S(1)} %pad_maximum_fusion.rates, f32[96,2,2048]{2,1,0:T(2,128)S(1)} %copy-done.1), custom_call_target="tpu_custom_call" | custom-call | flops 10000000 | bytes 3145728 | tf_op jit(solution)/shard_map/pack/pallas_call | solution.py:87
  3.1 0.0 copy-start.2
  3.1 32.1 %all_to_all.10.received = bf16[16,104,256]{2,1,0:T(8,128)(2,1)S(1)} all-to-all(bf16[16,104,256]{2,1,0:T(8,128)(2,1)S(1)} %pack.1), channel_id=1, replica_groups=mesh['mode'=16,'cell'=32] {'mode'}, dimensions={0} | all-to-all | bytes 1703936 | tf_op jit(solution)/shard_map/all_to_all | solution.py:325
  35.1 0.5 unpack.1
  35.6 2.5 %collective-permute-start = (bf16[136,1536]{1,0:T(8,128)(2,1)S(1)}, bf16[136,1536]{1,0:T(8,128)(2,1)S(1)}, u32[]{:S(2)}, u32[]{:S(2)}) collective-permute-start(bf16[136,1536]{1,0:T(8,128)(2,1)S(1)} %get-tuple-element.15.own_0), channel_id=1, source_target_pairs={{0,1},{1,0},{2,3},{3,2},{4,5},{5,4},{6,7},{7,6},{8,9},{9,8},{10,11... | collective-permute-start | bytes 1253384 | tf_op jit(solution)/shard_map/ppermute | solution.py:22
  38.1 5.8 %collective-permute-start.1 = (bf16[136,1536]{1,0:T(8,128)(2,1)S(1)}, bf16[136,1536]{1,0:T(8,128)(2,1)S(1)}, u32[]{:S(2)}, u32[]{:S(2)}) collective-permute-start(bf16[136,1536]{1,0:T(8,128)(2,1)S(1)} %get-tuple-element.16.own_1), channel_id=1, source_target_pairs={{1,2},{2,1},{3,4},{4,3},{5,6},{6,5},{7,8},{8,7},{9,10},{10,9},{11,... | collective-permute-start | bytes 1253384 | tf_op jit(solution)/shard_map/ppermute | solution.py:23
  43.9 0.0 copy-done
  43.9 0.0 copy-done.2
  43.9 2.1 %first_step.1 = (f32[136,1536]{1,0:T(8,128)S(1)}, f32[136,1536]{1,0:T(8,128)S(1)}, bf16[128,1536]{1,0:T(8,128)(2,1)S(1)}, bf16[128,1536]{1,0:T(8,128)(2,1)S(1)}, f32[136,8]{1,0:T(8,128)S(1)}) custom-call(bf16[136,1536]{1,0:T(8,128)(2,1)S(1)} %get-tuple-element.15.own_0, bf16[136,1536]{1,0:T(8,128)(2,1)S(1)} %get-tuple-element.16.own_1, ...), custom_call_target="tpu_custom_call" | custom-call | flops 1283457024 | bytes 8388608 | tf_op jit(solution)/shard_map/first_step/pallas_call | solution.py:199
  46.0 1.9 %collective-permute-start.2 = (bf16[128,1536]{1,0:T(8,128)(2,1)S(1)}, bf16[128,1536]{1,0:T(8,128)(2,1)S(1)}, u32[]{:S(2)}, u32[]{:S(2)}) collective-permute-start(bf16[128,1536]{1,0:T(8,128)(2,1)S(1)} %get-tuple-element.23), channel_id=1, source_target_pairs={{0,1},{1,0},{2,3},{3,2},{4,5},{5,4},{6,7},{7,6},{8,9},{9,8},{10,11... | collective-permute-start | bytes 1179656 | tf_op jit(solution)/shard_map/ppermute | solution.py:22
  47.9 4.0 %collective-permute-start.3 = (bf16[128,1536]{1,0:T(8,128)(2,1)S(1)}, bf16[128,1536]{1,0:T(8,128)(2,1)S(1)}, u32[]{:S(2)}, u32[]{:S(2)}) collective-permute-start(bf16[128,1536]{1,0:T(8,128)(2,1)S(1)} %get-tuple-element.24), channel_id=1, source_target_pairs={{1,2},{2,1},{3,4},{4,3},{5,6},{6,5},{7,8},{8,7},{9,10},{10,9},{11,... | collective-permute-start | bytes 1179656 | tf_op jit(solution)/shard_map/ppermute | solution.py:23
  52.0 0.0 collective-permute-done.near_0
  52.0 2.9 %collective-permute-done.1.near_1 = bf16[136,1536]{1,0:T(8,128)(2,1)S(1)} collective-permute-done((bf16[136,1536]{1,0:T(8,128)(2,1)S(1)}, bf16[136,1536]{1,0:T(8,128)(2,1)S(1)}, u32[]{:S(2)}, u32[]{:S(2)}) %collective-permute-start.1) | collective-permute-done | bytes 417824 | tf_op jit(solution)/shard_map/ppermute | solution.py:23
  54.9 1.9 %second_step.1 = (f32[128,1536]{1,0:T(8,128)S(1)}, f32[128,1536]{1,0:T(8,128)S(1)}) custom-call(f32[136,1536]{1,0:T(8,128)S(1)} %get-tuple-element.18.part_0, f32[136,1536]{1,0:T(8,128)S(1)} %get-tuple-element.19.part_1, bf16[136,1536]{1,0:T(8,128)(2,1)S(1)} %collective-permute-done.near_0, bf16[136,1536]{1,0:T(8,128)(2,1)S(1)} %collective-permute-done.1.near_1, ...), custom_call_target="tpu_custom_call" | custom-call | flops 1283457024 | bytes 8388608 | tf_op jit(solution)/shard_map/second_step/pallas_call | solution.py:238
  56.8 2.0 %collective-permute-done.2.near_0 = bf16[128,1536]{1,0:T(8,128)(2,1)S(1)} collective-permute-done((bf16[128,1536]{1,0:T(8,128)(2,1)S(1)}, bf16[128,1536]{1,0:T(8,128)(2,1)S(1)}, u32[]{:S(2)}, u32[]{:S(2)}) %collective-permute-start.2) | collective-permute-done | bytes 393248 | tf_op jit(solution)/shard_map/ppermute | solution.py:22
  58.7 5.2 %collective-permute-done.3.near_1 = bf16[128,1536]{1,0:T(8,128)(2,1)S(1)} collective-permute-done((bf16[128,1536]{1,0:T(8,128)(2,1)S(1)}, bf16[128,1536]{1,0:T(8,128)(2,1)S(1)}, u32[]{:S(2)}, u32[]{:S(2)}) %collective-permute-start.3) | collective-permute-done | bytes 393248 | tf_op jit(solution)/shard_map/ppermute | solution.py:23
  64.0 0.4 finish.1
  64.4 26.3 %all_to_all.11.result = bf16[16,96,256]{2,1,0:T(8,128)(2,1)S(1)} all-to-all(bf16[16,96,256]{2,1,0:T(8,128)(2,1)S(1)} %finish.1), channel_id=1, replica_groups=mesh['mode'=16,'cell'=32] {'mode'}, dimensions={0} | all-to-all | bytes 1572864 | tf_op jit(solution)/shard_map/all_to_all | solution.py:332
  90.7 1.5 %spread.1 = f32[96,2,2048]{2,1,0:T(2,128)} custom-call(bf16[16,96,256]{2,1,0:T(8,128)(2,1)S(1)} %all_to_all.11.result), custom_call_target="tpu_custom_call" | custom-call | flops 10000000 | bytes 3145728 | tf_op jit(solution)/shard_map/spread/pallas_call | solution.py:307
Async XLA Ops:
  0.7 1.4 %copy-start.1 = (f32[96,2,2048]{2,1,0:T(2,128)S(1)}, f32[96,2,2048]{2,1,0:T(2,128)}, u32[]{:S(2)}) copy-start(f32[96,2,2048]{2,1,0:T(2,128)} %initial.1) | copy-start | bytes 4718596
  2.1 41.8 %copy-start = (bf16[1536,1536]{1,0:T(8,128)(2,1)S(1)}, bf16[1536,1536]{1,0:T(8,128)(2,1)}, u32[]{:S(2)}) copy-start(bf16[1536,1536]{1,0:T(8,128)(2,1)} %matrix.3) | copy-start | bytes 14155780
  3.1 40.8 %copy-start.2 = (s32[2,2048]{1,0:T(2,128)S(1)}, s32[2,2048]{1,0:T(2,128)}, u32[]{:S(2)}) copy-start(s32[2,2048]{1,0:T(2,128)} %heater.1) | copy-start | bytes 49156
  35.6 16.4 %collective-permute-start = (bf16[136,1536]{1,0:T(8,128)(2,1)S(1)}, bf16[136,1536]{1,0:T(8,128)(2,1)S(1)}, u32[]{:S(2)}, u32[]{:S(2)}) collective-permute-start(bf16[136,1536]{1,0:T(8,128)(2,1)S(1)} %get-tuple-element.15.own_0), channel_id=1, source_target_pairs={{0,1},{1,0},{2,3},{3,2},{4,5},{5,4},{6,7},{7,6},{8,9},{9,8},{10,11... | collective-permute-start | bytes 1253384 | tf_op jit(solution)/shard_map/ppermute | solution.py:22
  38.1 16.8 %collective-permute-start.1 = (bf16[136,1536]{1,0:T(8,128)(2,1)S(1)}, bf16[136,1536]{1,0:T(8,128)(2,1)S(1)}, u32[]{:S(2)}, u32[]{:S(2)}) collective-permute-start(bf16[136,1536]{1,0:T(8,128)(2,1)S(1)} %get-tuple-element.16.own_1), channel_id=1, source_target_pairs={{1,2},{2,1},{3,4},{4,3},{5,6},{6,5},{7,8},{8,7},{9,10},{10,9},{11,... | collective-permute-start | bytes 1253384 | tf_op jit(solution)/shard_map/ppermute | solution.py:23
  46.0 12.7 %collective-permute-start.2 = (bf16[128,1536]{1,0:T(8,128)(2,1)S(1)}, bf16[128,1536]{1,0:T(8,128)(2,1)S(1)}, u32[]{:S(2)}, u32[]{:S(2)}) collective-permute-start(bf16[128,1536]{1,0:T(8,128)(2,1)S(1)} %get-tuple-element.23), channel_id=1, source_target_pairs={{0,1},{1,0},{2,3},{3,2},{4,5},{5,4},{6,7},{7,6},{8,9},{9,8},{10,11... | collective-permute-start | bytes 1179656 | tf_op jit(solution)/shard_map/ppermute | solution.py:22
  47.9 16.0 %collective-permute-start.3 = (bf16[128,1536]{1,0:T(8,128)(2,1)S(1)}, bf16[128,1536]{1,0:T(8,128)(2,1)S(1)}, u32[]{:S(2)}, u32[]{:S(2)}) collective-permute-start(bf16[128,1536]{1,0:T(8,128)(2,1)S(1)} %get-tuple-element.24), channel_id=1, source_target_pairs={{1,2},{2,1},{3,4},{4,3},{5,6},{6,5},{7,8},{8,7},{9,10},{10,9},{11,... | collective-permute-start | bytes 1179656 | tf_op jit(solution)/shard_map/ppermute | solution.py:23

commit v6 on v5

--- a/solution.py
+++ b/solution.py
@@ -10,7 +10,7 @@
 SIDE = 8
 TILE = 256
 MIB = 1024 * 1024
-PIECES = 4
+PIECES = 8
 
 
 def swap(to_first, to_second):
@@ -95,23 +95,17 @@
     )(rates, initial)
 
 
-def unpack_body(received, own_0, own_1, coef):
+def unpack_body(received, own_0, own_1):
     groups, height, cells = received.shape
     modes, span = height - SIDE, cells // 2
     unit = one_hot(iota((span, span), 0) == iota((span, span), 1))
     even = lax.axis_index("cell") % 2 == 0
-    together = 4
+    together = 8
     wide = together * modes
     for first in range(0, groups, together):
         lanes = pl.ds(first // together * wide, wide)
         members = range(first, first + together)
         edge = jnp.concatenate([received[j, modes:, :modes] for j in members], axis=1).astype(F32)
-        vector = jnp.concatenate(
-            [received[j, modes:, span : span + modes] for j in members], axis=1
-        ).astype(F32)
-        vector = vector + pltpu.roll(vector, 4, 0)
-        sign = jnp.where((iota((SIDE, wide), 0) == 0) & jnp.logical_not(even), -1.0, 1.0)
-        coef[:, lanes] = vector * sign
         other = pltpu.roll(edge, 4, 0)
         for c, out in ((0, own_0), (1, own_1)):
             column = jnp.where(even, 1 - c, c)
@@ -130,9 +124,8 @@
     return pl.pallas_call(
         unpack_body,
         in_specs=[IN_VMEM],
-        out_specs=[IN_VMEM] * 3,
-        out_shape=[jax.ShapeDtypeStruct((rows, total), BF16)] * 2
-        + [jax.ShapeDtypeStruct((SIDE, total), F32)],
+        out_specs=[IN_VMEM] * 2,
+        out_shape=[jax.ShapeDtypeStruct((rows, total), BF16)] * 2,
         compiler_params=params(24),
         cost_estimate=pl.CostEstimate(flops=10**7, bytes_accessed=3 * MIB, transcendentals=0),
         name="unpack",
@@ -157,12 +150,24 @@
     )
 
 
-def first_body(own_0, own_1, matrix, coef, heater, part_0, part_1, sent_0, sent_1, heat, both):
+def first_body(own_0, own_1, matrix, received, heater, part_0, part_1, sent_0, sent_1, heat, coef, both):
     rows, total = own_0.shape
     span = rows - SIDE
-    groups = heater.shape[1] // span
+    groups, height, _ = received.shape
+    modes = height - SIDE
+    together = 4
+    wide = together * modes
+    even = lax.axis_index("cell") % 2 == 0
+    for first in range(0, groups, together):
+        lanes = pl.ds(first // together * wide, wide)
+        members = range(first, first + together)
+        vector = jnp.concatenate(
+            [received[j, modes:, span : span + modes] for j in members], axis=1
+        ).astype(F32)
+        vector = vector + pltpu.roll(vector, 4, 0)
+        sign = jnp.where((iota((SIDE, wide), 0) == 0) & jnp.logical_not(even), -1.0, 1.0)
+        coef[:, lanes] = vector * sign
     me = lax.axis_index("mode")
-    even = lax.axis_index("cell") % 2 == 0
     parts = []
     for k in (-1, 0, 1):
         there = me + k
@@ -194,22 +199,22 @@
         sent_1[:, at] = value[:span].astype(BF16)
 
 
-def first_step(own_0, own_1, matrix, coef, heater):
+def first_step(own_0, own_1, matrix, received, heater):
     rows, total = own_0.shape
     return pl.pallas_call(
         first_body,
         in_specs=[IN_VMEM] * 5,
-        out_specs=[IN_VMEM] * 5,
+        out_specs=[IN_VMEM] * 6,
         out_shape=[jax.ShapeDtypeStruct((rows, total), F32)] * 2
         + [jax.ShapeDtypeStruct((rows - SIDE, total), BF16)] * 2
-        + [jax.ShapeDtypeStruct((rows, SIDE), F32)],
+        + [jax.ShapeDtypeStruct((rows, SIDE), F32), jax.ShapeDtypeStruct((SIDE, total), F32)],
         scratch_shapes=[pltpu.VMEM((2 * rows, total), BF16)],
         compiler_params=params(24),
         cost_estimate=pl.CostEstimate(
             flops=4 * rows * total * total, bytes_accessed=8 * MIB, transcendentals=0
         ),
         name="first_step",
-    )(own_0, own_1, matrix, coef, heater)
+    )(own_0, own_1, matrix, received, heater)
 
 
 def second_body(part_0, part_1, near_0, near_1, matrix, coef, heat, base_0, base_1, field, narrow):
@@ -323,9 +328,11 @@
 
     packed = pack(initial, jnp.stack([speed_x, speed_y, relaxation, emission]), groups)
     received = lax.all_to_all(packed, "mode", 0, 0, tiled=True)
-    own_0, own_1, coef = unpack(received)
+    own_0, own_1 = unpack(received)
     near_0, near_1 = swap(own_0, own_1)
-    part_0, part_1, sent_0, sent_1, heat = first_step(own_0, own_1, scatter_matrix, coef, heater)
+    part_0, part_1, sent_0, sent_1, heat, coef = first_step(
+        own_0, own_1, scatter_matrix, received, heater
+    )
     far_0, far_1 = swap(sent_0, sent_1)
     base_0, base_1 = second_step(part_0, part_1, near_0, near_1, scatter_matrix, coef, heat)
     result = finish(base_0, base_1, far_0, far_1, coef, groups)

time: 92.4 us -> 92.2 us (level)
  no operation moved by 1% of the time
where the time goes in v6:
time: 92.2 us; the launch traced here: 91.9 us
  blocking collectives  58.3 us (63%)
  starting transfers between devices  14.2 us (15%)
  waiting for transfers between devices  10.1 us (11%)
  Pallas kernels  7.1 us (8%)
  local copies, waits for them, and re-layouts  1.41 us (2%)
    all_to_all x1, blocking collectives, shards(): received = lax.all_to_all(packed, 'mode', 0, 0, tiled=True)  32.1 us
    all_to_all x1, blocking collectives, shards(): result = lax.all_to_all(result, 'mode', 0, 0, tiled=True)  26.3 us
    ppermute x2, starting transfers between devices, swap(): lax.ppermute(to_second, 'cell', inside(second))  9.82 us
    ppermute x2, waiting for transfers between devices, swap(): lax.ppermute(to_second, 'cell', inside(second))  8.18 us
    ppermute x2, starting transfers between devices, swap(): lax.ppermute(to_first, 'cell', inside(first))  4.37 us
    pallas_call x1, Pallas kernels, first_step(): pl.pallas_call(first_body, in_specs=[IN_VMEM] * 5, out_specs=[IN_VMEM] *...  2.04 us
    pallas_call x1, Pallas kernels, second_step(): pl.pallas_call(second_body, in_specs=[IN_VMEM] * 7, out_specs=[IN_VMEM] *...  1.94 us
    ppermute x2, waiting for transfers between devices, swap(): lax.ppermute(to_first, 'cell', inside(first))  1.88 us
  transfers between devices with their start and end apart: 4, of which 3 were waited for; matrix products, arithmetic and copies ran while one was open for 0% of the time, Pallas kernels for 4%

profile of v6, /device:TPU:199, one launch (start us, length us, event | category | flops | bytes accessed | tf_op | source)
XLA Modules:
  0.0 91.9 jit_solution(13733985053913444230)
XLA Ops:
  0.0 0.7 pad_maximum_fusion.rates
  0.7 0.0 copy-start.1
  0.7 1.4 %copy-done.1 = f32[96,2,2048]{2,1,0:T(2,128)S(1)} copy-done((f32[96,2,2048]{2,1,0:T(2,128)S(1)}, f32[96,2,2048]{2,1,0:T(2,128)}, u32[]{:S(2)}) %copy-start.1) | copy-done | bytes 1572888
  2.1 0.0 copy-start
  2.1 0.9 pack.1
  3.0 0.0 copy-start.2
  3.0 32.1 %all_to_all.10.received = bf16[16,104,256]{2,1,0:T(8,128)(2,1)S(1)} all-to-all(bf16[16,104,256]{2,1,0:T(8,128)(2,1)S(1)} %pack.1), channel_id=1, replica_groups=mesh['mode'=16,'cell'=32] {'mode'}, dimensions={0} | all-to-all | bytes 1703936 | tf_op jit(solution)/shard_map/all_to_all | solution.py:330
  35.1 0.4 unpack.1
  35.5 2.5 %collective-permute-start = (bf16[136,1536]{1,0:T(8,128)(2,1)S(1)}, bf16[136,1536]{1,0:T(8,128)(2,1)S(1)}, u32[]{:S(2)}, u32[]{:S(2)}) collective-permute-start(bf16[136,1536]{1,0:T(8,128)(2,1)S(1)} %get-tuple-element.15.own_0), channel_id=1, source_target_pairs={{0,1},{1,0},{2,3},{3,2},{4,5},{5,4},{6,7},{7,6},{8,9},{9,8},{10,11... | collective-permute-start | bytes 1253384 | tf_op jit(solution)/shard_map/ppermute | solution.py:22
  37.9 5.8 %collective-permute-start.1 = (bf16[136,1536]{1,0:T(8,128)(2,1)S(1)}, bf16[136,1536]{1,0:T(8,128)(2,1)S(1)}, u32[]{:S(2)}, u32[]{:S(2)}) collective-permute-start(bf16[136,1536]{1,0:T(8,128)(2,1)S(1)} %get-tuple-element.16.own_1), channel_id=1, source_target_pairs={{1,2},{2,1},{3,4},{4,3},{5,6},{6,5},{7,8},{8,7},{9,10},{10,9},{11,... | collective-permute-start | bytes 1253384 | tf_op jit(solution)/shard_map/ppermute | solution.py:23
  43.7 0.0 copy-done
  43.7 0.0 copy-done.2
  43.8 2.0 %first_step.1 = (f32[136,1536]{1,0:T(8,128)S(1)}, f32[136,1536]{1,0:T(8,128)S(1)}, bf16[128,1536]{1,0:T(8,128)(2,1)S(1)}, bf16[128,1536]{1,0:T(8,128)(2,1)S(1)},...) custom-call(bf16[136,1536]{1,0:T(8,128)(2,1)S(1)} %get-tuple-element.15.own_0, ...), custom_call_target="tpu_custom_call" | custom-call | flops 1283457024 | bytes 8388608 | tf_op jit(solution)/shard_map/first_step/pallas_call | solution.py:204
  45.8 1.9 %collective-permute-start.2 = (bf16[128,1536]{1,0:T(8,128)(2,1)S(1)}, bf16[128,1536]{1,0:T(8,128)(2,1)S(1)}, u32[]{:S(2)}, u32[]{:S(2)}) collective-permute-start(bf16[128,1536]{1,0:T(8,128)(2,1)S(1)} %get-tuple-element.23), channel_id=1, source_target_pairs={{0,1},{1,0},{2,3},{3,2},{4,5},{5,4},{6,7},{7,6},{8,9},{9,8},{10,11... | collective-permute-start | bytes 1179656 | tf_op jit(solution)/shard_map/ppermute | solution.py:22
  47.7 4.0 %collective-permute-start.3 = (bf16[128,1536]{1,0:T(8,128)(2,1)S(1)}, bf16[128,1536]{1,0:T(8,128)(2,1)S(1)}, u32[]{:S(2)}, u32[]{:S(2)}) collective-permute-start(bf16[128,1536]{1,0:T(8,128)(2,1)S(1)} %get-tuple-element.24), channel_id=1, source_target_pairs={{1,2},{2,1},{3,4},{4,3},{5,6},{6,5},{7,8},{8,7},{9,10},{10,9},{11,... | collective-permute-start | bytes 1179656 | tf_op jit(solution)/shard_map/ppermute | solution.py:23
  51.8 0.0 collective-permute-done.near_0
  51.8 2.9 %collective-permute-done.1.near_1 = bf16[136,1536]{1,0:T(8,128)(2,1)S(1)} collective-permute-done((bf16[136,1536]{1,0:T(8,128)(2,1)S(1)}, bf16[136,1536]{1,0:T(8,128)(2,1)S(1)}, u32[]{:S(2)}, u32[]{:S(2)}) %collective-permute-start.1) | collective-permute-done | bytes 417824 | tf_op jit(solution)/shard_map/ppermute | solution.py:23
  54.7 1.9 %second_step.1 = (f32[128,1536]{1,0:T(8,128)S(1)}, f32[128,1536]{1,0:T(8,128)S(1)}) custom-call(f32[136,1536]{1,0:T(8,128)S(1)} %get-tuple-element.17.part_0, f32[136,1536]{1,0:T(8,128)S(1)} %get-tuple-element.18.part_1, bf16[136,1536]{1,0:T(8,128)(2,1)S(1)} %collective-permute-done.near_0, bf16[136,1536]{1,0:T(8,128)(2,1)S(1)} %collective-permute-done.1.near_1, ...), custom_call_target="tpu_custom_call" | custom-call | flops 1283457024 | bytes 8388608 | tf_op jit(solution)/shard_map/second_step/pallas_call | solution.py:243
  56.7 1.9 %collective-permute-done.2.near_0 = bf16[128,1536]{1,0:T(8,128)(2,1)S(1)} collective-permute-done((bf16[128,1536]{1,0:T(8,128)(2,1)S(1)}, bf16[128,1536]{1,0:T(8,128)(2,1)S(1)}, u32[]{:S(2)}, u32[]{:S(2)}) %collective-permute-start.2) | collective-permute-done | bytes 393248 | tf_op jit(solution)/shard_map/ppermute | solution.py:22
  58.5 5.2 %collective-permute-done.3.near_1 = bf16[128,1536]{1,0:T(8,128)(2,1)S(1)} collective-permute-done((bf16[128,1536]{1,0:T(8,128)(2,1)S(1)}, bf16[128,1536]{1,0:T(8,128)(2,1)S(1)}, u32[]{:S(2)}, u32[]{:S(2)}) %collective-permute-start.3) | collective-permute-done | bytes 393248 | tf_op jit(solution)/shard_map/ppermute | solution.py:23
  63.8 0.4 finish.1
  64.2 26.3 %all_to_all.11.result = bf16[16,96,256]{2,1,0:T(8,128)(2,1)S(1)} all-to-all(bf16[16,96,256]{2,1,0:T(8,128)(2,1)S(1)} %finish.1), channel_id=1, replica_groups=mesh['mode'=16,'cell'=32] {'mode'}, dimensions={0} | all-to-all | bytes 1572864 | tf_op jit(solution)/shard_map/all_to_all | solution.py:339
  90.5 1.4 %spread.1 = f32[96,2,2048]{2,1,0:T(2,128)} custom-call(bf16[16,96,256]{2,1,0:T(8,128)(2,1)S(1)} %all_to_all.11.result), custom_call_target="tpu_custom_call" | custom-call | flops 10000000 | bytes 3145728 | tf_op jit(solution)/shard_map/spread/pallas_call | solution.py:312
Async XLA Ops:
  0.7 1.4 %copy-start.1 = (f32[96,2,2048]{2,1,0:T(2,128)S(1)}, f32[96,2,2048]{2,1,0:T(2,128)}, u32[]{:S(2)}) copy-start(f32[96,2,2048]{2,1,0:T(2,128)} %initial.1) | copy-start | bytes 4718596
  2.1 41.6 %copy-start = (bf16[1536,1536]{1,0:T(8,128)(2,1)S(1)}, bf16[1536,1536]{1,0:T(8,128)(2,1)}, u32[]{:S(2)}) copy-start(bf16[1536,1536]{1,0:T(8,128)(2,1)} %matrix.3) | copy-start | bytes 14155780
  3.0 40.7 %copy-start.2 = (s32[2,2048]{1,0:T(2,128)S(1)}, s32[2,2048]{1,0:T(2,128)}, u32[]{:S(2)}) copy-start(s32[2,2048]{1,0:T(2,128)} %heater.1) | copy-start | bytes 49156
  35.5 16.3 %collective-permute-start = (bf16[136,1536]{1,0:T(8,128)(2,1)S(1)}, bf16[136,1536]{1,0:T(8,128)(2,1)S(1)}, u32[]{:S(2)}, u32[]{:S(2)}) collective-permute-start(bf16[136,1536]{1,0:T(8,128)(2,1)S(1)} %get-tuple-element.15.own_0), channel_id=1, source_target_pairs={{0,1},{1,0},{2,3},{3,2},{4,5},{5,4},{6,7},{7,6},{8,9},{9,8},{10,11... | collective-permute-start | bytes 1253384 | tf_op jit(solution)/shard_map/ppermute | solution.py:22
  37.9 16.8 %collective-permute-start.1 = (bf16[136,1536]{1,0:T(8,128)(2,1)S(1)}, bf16[136,1536]{1,0:T(8,128)(2,1)S(1)}, u32[]{:S(2)}, u32[]{:S(2)}) collective-permute-start(bf16[136,1536]{1,0:T(8,128)(2,1)S(1)} %get-tuple-element.16.own_1), channel_id=1, source_target_pairs={{1,2},{2,1},{3,4},{4,3},{5,6},{6,5},{7,8},{8,7},{9,10},{10,9},{11,... | collective-permute-start | bytes 1253384 | tf_op jit(solution)/shard_map/ppermute | solution.py:23
  45.8 12.7 %collective-permute-start.2 = (bf16[128,1536]{1,0:T(8,128)(2,1)S(1)}, bf16[128,1536]{1,0:T(8,128)(2,1)S(1)}, u32[]{:S(2)}, u32[]{:S(2)}) collective-permute-start(bf16[128,1536]{1,0:T(8,128)(2,1)S(1)} %get-tuple-element.23), channel_id=1, source_target_pairs={{0,1},{1,0},{2,3},{3,2},{4,5},{5,4},{6,7},{7,6},{8,9},{9,8},{10,11... | collective-permute-start | bytes 1179656 | tf_op jit(solution)/shard_map/ppermute | solution.py:22
  47.7 16.0 %collective-permute-start.3 = (bf16[128,1536]{1,0:T(8,128)(2,1)S(1)}, bf16[128,1536]{1,0:T(8,128)(2,1)S(1)}, u32[]{:S(2)}, u32[]{:S(2)}) collective-permute-start(bf16[128,1536]{1,0:T(8,128)(2,1)S(1)} %get-tuple-element.24), channel_id=1, source_target_pairs={{1,2},{2,1},{3,4},{4,3},{5,6},{6,5},{7,8},{8,7},{9,10},{10,9},{11,... | collective-permute-start | bytes 1179656 | tf_op jit(solution)/shard_map/ppermute | solution.py:23

commit v7 on v6

--- a/solution.py
+++ b/solution.py
@@ -180,8 +180,8 @@
     row, lane = iota((span + SIDE, 3 * span), 0), iota((span + SIDE, 3 * span), 1)
     pick = one_hot(lane == jnp.where(row < span + SIDE // 2, span + row, row - SIDE))
     heat[...] = lax.dot_general(pick, near, (((1,), (1,)), ((), ())), preferred_element_type=F32)
-    both[:rows, :] = own_0[...].astype(F32).astype(BF16)
-    both[rows:, :] = own_1[...].astype(F32).astype(BF16)
+    both[:rows, :] = own_0[...]
+    both[rows:, :] = own_1[...]
     for first in range(0, total, TILE):
         at = pl.ds(first, TILE)
         x_rate = coef[0:1, at]
@@ -295,11 +295,13 @@
     join = one_hot(row == jnp.where(lane < modes, 2 * lane, 2 * (lane - modes) + 1))
     copies = []
     for k in range(PIECES):
-        for group in range(k * per, (k + 1) * per):
-            both = jnp.concatenate([result[group, :, :span], result[group, :, span:]], axis=0)
-            both = jnp.dot(join, both, preferred_element_type=F32)
-            wide[:, :, pl.ds(group * span, span)] = both.reshape(modes, 2, span)
         at = pl.ds(k * per * span, per * span)
+        both = [
+            jnp.concatenate([result[group, :, :span], result[group, :, span:]], axis=0)
+            for group in range(k * per, (k + 1) * per)
+        ]
+        both = jnp.dot(join, jnp.concatenate(both, axis=1), preferred_element_type=F32)
+        wide[:, :, at] = both.reshape(modes, 2, per * span)
         copies.append(pltpu.make_async_copy(wide.at[:, :, at], out.at[:, :, at], sent.at[k]))
         copies[-1].start()
     for copy in copies:

time: 92.2 us -> 92.2 us (level)
  no operation moved by 1% of the time
where the time goes in v7:
time: 92.2 us; the launch traced here: 91.9 us
  blocking collectives  58.3 us (63%)
  starting transfers between devices  14.2 us (15%)
  waiting for transfers between devices  10.1 us (11%)
  Pallas kernels  7.11 us (8%)
  local copies, waits for them, and re-layouts  1.41 us (2%)
    all_to_all x1, blocking collectives, shards(): received = lax.all_to_all(packed, 'mode', 0, 0, tiled=True)  32.1 us
    all_to_all x1, blocking collectives, shards(): result = lax.all_to_all(result, 'mode', 0, 0, tiled=True)  26.3 us
    ppermute x2, starting transfers between devices, swap(): lax.ppermute(to_second, 'cell', inside(second))  9.82 us
    ppermute x2, waiting for transfers between devices, swap(): lax.ppermute(to_second, 'cell', inside(second))  8.18 us
    ppermute x2, starting transfers between devices, swap(): lax.ppermute(to_first, 'cell', inside(first))  4.37 us
    pallas_call x1, Pallas kernels, first_step(): pl.pallas_call(first_body, in_specs=[IN_VMEM] * 5, out_specs=[IN_VMEM] *...  2.04 us
    pallas_call x1, Pallas kernels, second_step(): pl.pallas_call(second_body, in_specs=[IN_VMEM] * 7, out_specs=[IN_VMEM] *...  1.94 us
    ppermute x2, waiting for transfers between devices, swap(): lax.ppermute(to_first, 'cell', inside(first))  1.88 us
  transfers between devices with their start and end apart: 4, of which 3 were waited for; matrix products, arithmetic and copies ran while one was open for 0% of the time, Pallas kernels for 4%

profile of v7, /device:TPU:199, one launch (start us, length us, event | category | flops | bytes accessed | tf_op | source)
XLA Modules:
  0.0 91.9 jit_solution(5169443487160706305)
XLA Ops:
  0.0 0.7 pad_maximum_fusion.rates
  0.7 0.0 copy-start.1
  0.7 1.4 %copy-done.1 = f32[96,2,2048]{2,1,0:T(2,128)S(1)} copy-done((f32[96,2,2048]{2,1,0:T(2,128)S(1)}, f32[96,2,2048]{2,1,0:T(2,128)}, u32[]{:S(2)}) %copy-start.1) | copy-done | bytes 1572888
  2.1 0.0 copy-start
  2.1 0.9 pack.1
  3.0 0.0 copy-start.2
  3.0 32.1 %all_to_all.10.received = bf16[16,104,256]{2,1,0:T(8,128)(2,1)S(1)} all-to-all(bf16[16,104,256]{2,1,0:T(8,128)(2,1)S(1)} %pack.1), channel_id=1, replica_groups=mesh['mode'=16,'cell'=32] {'mode'}, dimensions={0} | all-to-all | bytes 1703936 | tf_op jit(solution)/shard_map/all_to_all | solution.py:332
  35.1 0.4 unpack.1
  35.5 2.5 %collective-permute-start = (bf16[136,1536]{1,0:T(8,128)(2,1)S(1)}, bf16[136,1536]{1,0:T(8,128)(2,1)S(1)}, u32[]{:S(2)}, u32[]{:S(2)}) collective-permute-start(bf16[136,1536]{1,0:T(8,128)(2,1)S(1)} %get-tuple-element.15.own_0), channel_id=1, source_target_pairs={{0,1},{1,0},{2,3},{3,2},{4,5},{5,4},{6,7},{7,6},{8,9},{9,8},{10,11... | collective-permute-start | bytes 1253384 | tf_op jit(solution)/shard_map/ppermute | solution.py:22
  37.9 5.8 %collective-permute-start.1 = (bf16[136,1536]{1,0:T(8,128)(2,1)S(1)}, bf16[136,1536]{1,0:T(8,128)(2,1)S(1)}, u32[]{:S(2)}, u32[]{:S(2)}) collective-permute-start(bf16[136,1536]{1,0:T(8,128)(2,1)S(1)} %get-tuple-element.16.own_1), channel_id=1, source_target_pairs={{1,2},{2,1},{3,4},{4,3},{5,6},{6,5},{7,8},{8,7},{9,10},{10,9},{11,... | collective-permute-start | bytes 1253384 | tf_op jit(solution)/shard_map/ppermute | solution.py:23
  43.7 0.0 copy-done
  43.7 0.0 copy-done.2
  43.8 2.0 %first_step.1 = (f32[136,1536]{1,0:T(8,128)S(1)}, f32[136,1536]{1,0:T(8,128)S(1)}, bf16[128,1536]{1,0:T(8,128)(2,1)S(1)}, bf16[128,1536]{1,0:T(8,128)(2,1)S(1)},...) custom-call(bf16[136,1536]{1,0:T(8,128)(2,1)S(1)} %get-tuple-element.15.own_0, ...), custom_call_target="tpu_custom_call" | custom-call | flops 1283457024 | bytes 8388608 | tf_op jit(solution)/shard_map/first_step/pallas_call | solution.py:204
  45.8 1.9 %collective-permute-start.2 = (bf16[128,1536]{1,0:T(8,128)(2,1)S(1)}, bf16[128,1536]{1,0:T(8,128)(2,1)S(1)}, u32[]{:S(2)}, u32[]{:S(2)}) collective-permute-start(bf16[128,1536]{1,0:T(8,128)(2,1)S(1)} %get-tuple-element.23), channel_id=1, source_target_pairs={{0,1},{1,0},{2,3},{3,2},{4,5},{5,4},{6,7},{7,6},{8,9},{9,8},{10,11... | collective-permute-start | bytes 1179656 | tf_op jit(solution)/shard_map/ppermute | solution.py:22
  47.7 4.0 %collective-permute-start.3 = (bf16[128,1536]{1,0:T(8,128)(2,1)S(1)}, bf16[128,1536]{1,0:T(8,128)(2,1)S(1)}, u32[]{:S(2)}, u32[]{:S(2)}) collective-permute-start(bf16[128,1536]{1,0:T(8,128)(2,1)S(1)} %get-tuple-element.24), channel_id=1, source_target_pairs={{1,2},{2,1},{3,4},{4,3},{5,6},{6,5},{7,8},{8,7},{9,10},{10,9},{11,... | collective-permute-start | bytes 1179656 | tf_op jit(solution)/shard_map/ppermute | solution.py:23
  51.8 0.0 collective-permute-done.near_0
  51.8 2.9 %collective-permute-done.1.near_1 = bf16[136,1536]{1,0:T(8,128)(2,1)S(1)} collective-permute-done((bf16[136,1536]{1,0:T(8,128)(2,1)S(1)}, bf16[136,1536]{1,0:T(8,128)(2,1)S(1)}, u32[]{:S(2)}, u32[]{:S(2)}) %collective-permute-start.1) | collective-permute-done | bytes 417824 | tf_op jit(solution)/shard_map/ppermute | solution.py:23
  54.7 1.9 %second_step.1 = (f32[128,1536]{1,0:T(8,128)S(1)}, f32[128,1536]{1,0:T(8,128)S(1)}) custom-call(f32[136,1536]{1,0:T(8,128)S(1)} %get-tuple-element.17.part_0, f32[136,1536]{1,0:T(8,128)S(1)} %get-tuple-element.18.part_1, bf16[136,1536]{1,0:T(8,128)(2,1)S(1)} %collective-permute-done.near_0, bf16[136,1536]{1,0:T(8,128)(2,1)S(1)} %collective-permute-done.1.near_1, ...), custom_call_target="tpu_custom_call" | custom-call | flops 1283457024 | bytes 8388608 | tf_op jit(solution)/shard_map/second_step/pallas_call | solution.py:243
  56.7 1.9 %collective-permute-done.2.near_0 = bf16[128,1536]{1,0:T(8,128)(2,1)S(1)} collective-permute-done((bf16[128,1536]{1,0:T(8,128)(2,1)S(1)}, bf16[128,1536]{1,0:T(8,128)(2,1)S(1)}, u32[]{:S(2)}, u32[]{:S(2)}) %collective-permute-start.2) | collective-permute-done | bytes 393248 | tf_op jit(solution)/shard_map/ppermute | solution.py:22
  58.5 5.2 %collective-permute-done.3.near_1 = bf16[128,1536]{1,0:T(8,128)(2,1)S(1)} collective-permute-done((bf16[128,1536]{1,0:T(8,128)(2,1)S(1)}, bf16[128,1536]{1,0:T(8,128)(2,1)S(1)}, u32[]{:S(2)}, u32[]{:S(2)}) %collective-permute-start.3) | collective-permute-done | bytes 393248 | tf_op jit(solution)/shard_map/ppermute | solution.py:23
  63.8 0.4 finish.1
  64.2 26.3 %all_to_all.11.result = bf16[16,96,256]{2,1,0:T(8,128)(2,1)S(1)} all-to-all(bf16[16,96,256]{2,1,0:T(8,128)(2,1)S(1)} %finish.1), channel_id=1, replica_groups=mesh['mode'=16,'cell'=32] {'mode'}, dimensions={0} | all-to-all | bytes 1572864 | tf_op jit(solution)/shard_map/all_to_all | solution.py:341
  90.5 1.4 %spread.1 = f32[96,2,2048]{2,1,0:T(2,128)} custom-call(bf16[16,96,256]{2,1,0:T(8,128)(2,1)S(1)} %all_to_all.11.result), custom_call_target="tpu_custom_call" | custom-call | flops 10000000 | bytes 3145728 | tf_op jit(solution)/shard_map/spread/pallas_call | solution.py:314
Async XLA Ops:
  0.7 1.4 %copy-start.1 = (f32[96,2,2048]{2,1,0:T(2,128)S(1)}, f32[96,2,2048]{2,1,0:T(2,128)}, u32[]{:S(2)}) copy-start(f32[96,2,2048]{2,1,0:T(2,128)} %initial.1) | copy-start | bytes 4718596
  2.1 41.6 %copy-start = (bf16[1536,1536]{1,0:T(8,128)(2,1)S(1)}, bf16[1536,1536]{1,0:T(8,128)(2,1)}, u32[]{:S(2)}) copy-start(bf16[1536,1536]{1,0:T(8,128)(2,1)} %matrix.3) | copy-start | bytes 14155780
  3.0 40.7 %copy-start.2 = (s32[2,2048]{1,0:T(2,128)S(1)}, s32[2,2048]{1,0:T(2,128)}, u32[]{:S(2)}) copy-start(s32[2,2048]{1,0:T(2,128)} %heater.1) | copy-start | bytes 49156
  35.5 16.3 %collective-permute-start = (bf16[136,1536]{1,0:T(8,128)(2,1)S(1)}, bf16[136,1536]{1,0:T(8,128)(2,1)S(1)}, u32[]{:S(2)}, u32[]{:S(2)}) collective-permute-start(bf16[136,1536]{1,0:T(8,128)(2,1)S(1)} %get-tuple-element.15.own_0), channel_id=1, source_target_pairs={{0,1},{1,0},{2,3},{3,2},{4,5},{5,4},{6,7},{7,6},{8,9},{9,8},{10,11... | collective-permute-start | bytes 1253384 | tf_op jit(solution)/shard_map/ppermute | solution.py:22
  37.9 16.8 %collective-permute-start.1 = (bf16[136,1536]{1,0:T(8,128)(2,1)S(1)}, bf16[136,1536]{1,0:T(8,128)(2,1)S(1)}, u32[]{:S(2)}, u32[]{:S(2)}) collective-permute-start(bf16[136,1536]{1,0:T(8,128)(2,1)S(1)} %get-tuple-element.16.own_1), channel_id=1, source_target_pairs={{1,2},{2,1},{3,4},{4,3},{5,6},{6,5},{7,8},{8,7},{9,10},{10,9},{11,... | collective-permute-start | bytes 1253384 | tf_op jit(solution)/shard_map/ppermute | solution.py:23
  45.8 12.7 %collective-permute-start.2 = (bf16[128,1536]{1,0:T(8,128)(2,1)S(1)}, bf16[128,1536]{1,0:T(8,128)(2,1)S(1)}, u32[]{:S(2)}, u32[]{:S(2)}) collective-permute-start(bf16[128,1536]{1,0:T(8,128)(2,1)S(1)} %get-tuple-element.23), channel_id=1, source_target_pairs={{0,1},{1,0},{2,3},{3,2},{4,5},{5,4},{6,7},{7,6},{8,9},{9,8},{10,11... | collective-permute-start | bytes 1179656 | tf_op jit(solution)/shard_map/ppermute | solution.py:22
  47.7 16.0 %collective-permute-start.3 = (bf16[128,1536]{1,0:T(8,128)(2,1)S(1)}, bf16[128,1536]{1,0:T(8,128)(2,1)S(1)}, u32[]{:S(2)}, u32[]{:S(2)}) collective-permute-start(bf16[128,1536]{1,0:T(8,128)(2,1)S(1)} %get-tuple-element.24), channel_id=1, source_target_pairs={{1,2},{2,1},{3,4},{4,3},{5,6},{6,5},{7,8},{8,7},{9,10},{10,9},{11,... | collective-permute-start | bytes 1179656 | tf_op jit(solution)/shard_map/ppermute | solution.py:23
